TPU v7x, 32 devices: a whole 2x2x4 slice. The times are simulated.
32 devices in a mesh: groups: 2 (over x), tensor: 4 (over y, core), dp: 4 (over z).
Axes of the slice: x: 2, y: 2, z: 4, core: 2. Of those that a mesh axis runs over, the one named last changes fastest.
Arguments:
- queries: bfloat16 [4096, 12288], P(('groups', 'dp'), 'tensor'), parts along dimension 0, may hold values from -24 to 24
- keys: bfloat16 [4096, 1024], P(('groups', 'dp')), parts along dimension 0, may hold values from -14 to 14
- values: bfloat16 [4096, 1024], P(('groups', 'dp')), parts along dimension 0, may hold values from -6 to 6
- page_start: int32 [4096], P(('groups', 'dp')), parts along dimension 0, may hold values from 0 to 2047, as said below
Outputs:
- gram_band: float32 [24576, 9216], P(('groups', 'tensor', 'dp')), parts along dimension 0
There are 2 independent parts, one for each index of `groups`. A program takes and returns all parts, laid end to end along the dimension named above; each array names one. Nothing has to cross between parts.
Inputs may be any that keep to these rules, and one draw needn't show every extreme that they name: p - page_start[p] < 512, page_start never falls and starts each page at its first position; some page has exactly 512 tokens, and pages cross from one run of 512 tokens into the next.
All inputs are finite; a program needn't handle non-finite values.
Results may differ from a plain program's by a relative error of at most 0.012.
Values may be sent and summed in bfloat16 or wider, within the bound.
No kernel may reach another device: no remote copies, remote signals or barrier semaphores. Data moves between devices by JAX's collectives and lax.ppermute only.
A program may use at most 256 MiB of HBM per device.

v0:
```python
import jax
import jax.numpy as jnp
from jax import lax
from jax.sharding import PartitionSpec as P

HEADS = 96
HD = 128
KV_HEADS = 8
PAGE = 512


def shifted(x, axis, by):
    devices = lax.axis_size(axis)
    pairs = [(i, i + by) for i in range(devices) if 0 <= i + by < devices]
    return lax.ppermute(x, axis, pairs)


def from_behind(value, axis, steps):
    count = lax.axis_size(axis)
    pairs = [(source, (source + steps) % count) for source in range(count)]
    return lax.ppermute(value, axis, pairs)


def per_device(queries, keys, values, page_start):
    tok_rows = queries.shape[0]
    slab_width = queries.shape[1]
    local_heads = slab_width // HD
    group = HEADS // KV_HEADS
    kv_count = max(1, local_heads // group)
    head_index = lax.axis_index("tensor")
    run_index = lax.axis_index("dp")
    kv_first = head_index * local_heads // group
    own_keys = lax.dynamic_slice_in_dim(keys, kv_first * HD, kv_count * HD, 1)
    own_values = lax.dynamic_slice_in_dim(values, kv_first * HD, kv_count * HD, 1)
    prev_keys, prev_values = shifted((own_keys, own_values), "dp", 1)
    ext_keys = jnp.concatenate([prev_keys, own_keys], 0)
    ext_values = jnp.concatenate([prev_values, own_values], 0)
    scale = 1.0 / HD**0.5
    per_kv = local_heads // kv_count
    base_pos = run_index * tok_rows
    query_rows = queries.reshape(PAGE, kv_count, per_kv, HD)
    key_rows = ext_keys.reshape(2 * PAGE, kv_count, HD)
    value_rows = ext_values.reshape(2 * PAGE, kv_count, HD)
    scores = (
        jnp.einsum("qkgd,skd->kgqs", query_rows, key_rows, preferred_element_type=jnp.float32)
        * scale
    )
    query_pos = base_pos + 0 + jnp.arange(PAGE, dtype=jnp.int32)
    key_pos = base_pos + 0 - PAGE + jnp.arange(2 * PAGE, dtype=jnp.int32)
    visible = (key_pos[None, :] >= page_start[:, None]) & (key_pos[None, :] <= query_pos[:, None])
    scores = jnp.where(visible[None, None], scores, -1e30)
    top = jnp.max(scores, axis=-1, keepdims=True)
    expo = jnp.exp(scores - top)
    probs = (expo / jnp.sum(expo, axis=-1, keepdims=True)).astype(jnp.bfloat16)
    mixed = jnp.einsum("kgqs,skd->qkgd", probs, value_rows, preferred_element_type=jnp.float32)
    outputs = mixed.reshape(PAGE, slab_width).astype(jnp.bfloat16)
    steps = lax.axis_size("tensor") // 2 + 1
    columns = [outputs]
    moving = outputs
    for offset in range(1, steps):
        moving = from_behind(moving, "tensor", -1)
        columns.append(moving)
    tiles = [
        lax.dot_general(
            outputs, other, (((0,), (0,)), ((), ())), preferred_element_type=jnp.float32
        )
        for other in columns
    ]
    summed = lax.psum_scatter(
        jnp.concatenate(tiles, 1).astype(jnp.bfloat16), "dp", scatter_dimension=0, tiled=True
    ).astype(jnp.float32)
    total_tokens = tok_rows * lax.axis_size("dp")
    return summed * (2.0 / total_tokens)


def solution(mesh):
    return jax.shard_map(
        per_device,
        mesh=mesh,
        in_specs=(
            P(("groups", "dp"), "tensor"),
            P(("groups", "dp"), None),
            P(("groups", "dp"), None),
            P(("groups", "dp")),
        ),
        out_specs=P(("groups", "tensor", "dp"), None),
        check_vma=False,
    )
```

profile of v0, /device:TPU:1, one launch (start us, length us, event | category | flops | bytes accessed | tf_op | source)
XLA Modules:
  0.0 1191.6 jit_solution(9337025978161944178)
XLA Ops:
  6.5 0.0 copy-start
  6.5 0.0 reduce-scatter.2.cloned.1.call-start
  6.5 1.2 copy-done
  7.8 0.1 copy.22
  7.9 4.0 collective-permute-start.1
  12.0 1.0 constant_dynamic-slice_fusion.1
  13.0 3.2 collective-permute-start
  16.2 4.6 copy.11
  20.9 1.2 compare_and_fusion
  22.0 0.5 collective-permute-done
  22.6 0.2 copy.9
  22.8 0.0 collective-permute-done.1
  22.8 0.1 pad_maximum_fusion.2
  22.9 26.1 %fusion.11 = (f32[2,12,512]{2,1,0:T(8,128)S(1)}, f32[2,12,512,1024]{2,3,1,0:T(8,128)}) fusion(pred[512,1024]{0,1:T(8,128)(4,1)S(1)} %compare_and_fusion, bf16[1024,2,128,1]{0,2,3,1:T(8,128)(2,1)S(1)} %bitcast.38, bf16[512,2,12,128]{0,3,2,1:T(8,128)(2,1)} %bitcast.36), kind=kOutput, calls=%fused_computation.25 | convolution fusion | flops 3271558144 | bytes 54575104 | tf_op jit(solution)/shard_map/sub | solution.py:53
  48.9 17.4 %fusion.8 = bf16[2,128,12,512]{3,1,2,0:T(8,128)(2,1)S(1)} fusion(bf16[1024,2,128,1]{0,2,3,1:T(8,128)(2,1)S(1)} %bitcast.37, f32[2,12,512,1024]{2,3,1,0:T(8,128)} %get-tuple-element.6, f32[2,12,512]{2,1,0:T(8,128)S(1)} %get-tuple-element.5), kind=kOutput, calls=%fused_computation.15 | convolution fusion | flops 3247964160 | bytes 54050816 | tf_op jit(solution)/shard_map/kgqs,skd->qkgd/dot_general | solution.py:55
  66.4 1.6 collective-permute-start.2
  67.9 36.1 %collective-permute-done.2 = bf16[512,3072]{0,1:T(8,128)(2,1)S(1)} collective-permute-done((bf16[512,3072]{0,1:T(8,128)(2,1)S(1)}, bf16[512,3072]{0,1:T(8,128)(2,1)S(1)}, u32[]{:S(2)}, u32[]{:S(2)}) %collective-permute-start.2) | collective-permute-done | bytes 3145760 | tf_op jit(solution)/shard_map/ppermute | solution.py:21
  104.0 0.0 collective-permute-start.3
  104.0 13.0 %convolution_convert_fusion.2 = bf16[3072,3072]{0,1:T(8,128)(2,1)} fusion(bf16[512,3072]{0,1:T(8,128)(2,1)S(1)} %bitcast.40), kind=kOutput, calls=%fused_computation.14 | convolution fusion | flops 9673113600 | bytes 22020096 | tf_op jit(solution)/shard_map/dot_general | solution.py:64
  117.0 13.0 %convolution_convert_fusion.1 = bf16[3072,3072]{0,1:T(8,128)(2,1)} fusion(bf16[512,3072]{0,1:T(8,128)(2,1)S(1)} %bitcast.41, bf16[512,3072]{0,1:T(8,128)(2,1)S(1)} %collective-permute-done.2), kind=kOutput, calls=%fused_computation.13 | convolution fusion | flops 9673113600 | bytes 25165824 | tf_op jit(solution)/shard_map/dot_general | solution.py:64
  130.0 10.8 collective-permute-done.3
  140.8 15.0 %convolution_convert_fusion = bf16[3072,3072]{0,1:T(8,128)(2,1)} fusion(bf16[512,3072]{0,1:T(8,128)(2,1)S(1)} %bitcast.42, bf16[512,3072]{0,1:T(8,128)(2,1)} %collective-permute-done.3), kind=kOutput, calls=%fused_computation.12 | convolution fusion | flops 9673113600 | bytes 25165824 | tf_op jit(solution)/shard_map/dot_general | solution.py:64
  155.9 62.3 %pad_maximum_fusion = bf16[3072,9216]{0,1:T(8,128)(2,1)} fusion(bf16[3072,3072]{0,1:T(8,128)(2,1)} %convolution_convert_fusion, bf16[3072,3072]{0,1:T(8,128)(2,1)} %convolution_convert_fusion.1, bf16[3072,3072]{0,1:T(8,128)(2,1)} %convolution_convert_fusion.2), kind=kLoop, calls=%fused_computation.1 | loop fusion | flops 169869312 | bytes 113246208 | tf_op jit(solution)/shard_map/concatenate | solution.py:70
  218.2 0.0 reduce-scatter.2.cloned.1.call-update
  218.2 923.0 %reduce-scatter.2.cloned.1.call-done = bf16[768,9216]{0,1:T(8,128)(2,1)} async-done(((bf16[3072,9216]{0,1:T(8,128)(2,1)}), bf16[768,9216]{0,1:T(8,128)(2,1)}) %reduce-scatter.2.cloned.1.call-update) | async-done | bytes 14155792 | tf_op jit(solution)/shard_map/reduce_scatter | solution.py:69
  1141.2 0.0 copy-start.1
  1141.2 15.9 %convert_multiply_fusion = f32[768,9216]{0,1:T(8,128)} fusion(bf16[768,9216]{0,1:T(8,128)(2,1)} %reduce-scatter.2.cloned.1.call-done), kind=kLoop, calls=%fused_computation.6 | loop fusion | flops 14155776 | bytes 42467328 | tf_op jit(solution)/shard_map/mul | solution.py:73
  1157.0 27.7 %copy.15 = f32[768,9216]{1,0:T(8,128)} copy(f32[768,9216]{0,1:T(8,128)} %convert_multiply_fusion) | data formatting | bytes 56623104 | tf_op jit(solution)/shard_map/mul | solution.py:73
  1184.8 0.0 copy-done.1
  (4 shorter events, 0.1 us)
Async XLA Ops:
  6.5 1.2 copy-start
  6.5 1134.6 %reduce-scatter.2.cloned.1.call-start = ((), (), s32[]{:S(2)}) async-start(), calls=%async_computation.1 | async-start | bytes 70778880 | tf_op jit(solution)/shard_map/reduce_scatter | solution.py:69
  7.9 14.9 %collective-permute-start.1 = (bf16[512,256]{0,1:T(8,128)(2,1)S(1)}, bf16[512,256]{0,1:T(8,128)(2,1)S(1)}, u32[]{:S(2)}, u32[]{:S(2)}) collective-permute-start(bf16[512,256]{0,1:T(8,128)(2,1)S(1)} %copy.22), channel_id=1, source_target_pairs={{0,1},{1,2},{2,3},{4,5},{5,6},{6,7},{8,9},{9,10},{10,11},{12,13},{... | collective-permute-start | bytes 786440 | tf_op jit(solution)/shard_map/ppermute | solution.py:15
  13.0 9.6 collective-permute-start
  66.4 37.7 %collective-permute-start.2 = (bf16[512,3072]{0,1:T(8,128)(2,1)S(1)}, bf16[512,3072]{0,1:T(8,128)(2,1)S(1)}, u32[]{:S(2)}, u32[]{:S(2)}) collective-permute-start(bf16[512,3072]{0,1:T(8,128)(2,1)S(1)} %bitcast.39), channel_id=1, source_target_pairs={{0,12},{4,0},{8,4},{12,8},{1,13},{5,1},{9,5},{13,9},{2,14},{6,2},{... | collective-permute-start | bytes 9437192 | tf_op jit(solution)/shard_map/ppermute | solution.py:21
  104.0 36.8 %collective-permute-start.3 = (bf16[512,3072]{0,1:T(8,128)(2,1)S(1)}, bf16[512,3072]{0,1:T(8,128)(2,1)}, u32[]{:S(2)}, u32[]{:S(2)}) collective-permute-start(bf16[512,3072]{0,1:T(8,128)(2,1)S(1)} %collective-permute-done.2), channel_id=1, source_target_pairs={{0,12},{4,0},{8,4},{12,8},{1,13},{5,1},{9,5},{13,9},{2,14},{6,2},{... | collective-permute-start | bytes 9437192 | tf_op jit(solution)/shard_map/ppermute | solution.py:21
  1141.2 43.6 %copy-start.1 = (bf16[512,1024]{1,0:T(8,128)(2,1)S(1)}, bf16[512,1024]{1,0:T(8,128)(2,1)}, u32[]{:S(2)}) copy-start(bf16[512,1024]{1,0:T(8,128)(2,1)} %param.5) | copy-start | bytes 3145732
Sparse Core Ops, SparseCore 0:
  218.3 922.7 reduce-scatter.1
where the time goes:
time: 1190 us
  waiting for transfers between devices  970 us (82%)
  matrix products  84.5 us (7%)
  other arithmetic  79.4 us (7%)
  local copies, waits for them, and re-layouts  34.9 us (3%)
  between operations  13.5 us (1%)
    reduce_scatter x1, waiting for transfers between devices, per_device(): lax.psum_scatter(jnp.concatenate(tiles, 1).astype(jnp.bfloat16), 'dp', sc...  923 us
    concatenate x1, other arithmetic, per_device(): jnp.concatenate(tiles, 1).astype(jnp.bfloat16)  62.3 us
    ppermute x2, waiting for transfers between devices, from_behind(): return lax.ppermute(value, axis, pairs)  46.9 us
    dot_general x3, matrix products, per_device(): lax.dot_general(outputs, other, (((0,), (0,)), ((), ())), preferred_eleme...  41 us
    mul x1, local copies, waits for them, and re-layouts, per_device(): return summed * (2.0 / total_tokens)  27.7 us
    sub x1, matrix products, per_device(): expo = jnp.exp(scores - top)  26.1 us
  transfers between devices with their start and end apart: 5, of which 4 were waited for; matrix products, arithmetic and copies ran while one was open for 3% of the time, Pallas kernels for 0%

commit v1 on v0

v1 whole, which is shorter than its diff:
```python
import functools

import jax
import jax.numpy as jnp
from jax import lax
from jax.experimental import pallas as pl
from jax.experimental.pallas import tpu as pltpu
from jax.sharding import PartitionSpec as P

HEADS = 96
HD = 128
KV_HEADS = 8
PAGE = 512
TILE = 256
LOG2E = 1.4426950408889634
VMEM_LIMIT = 56 * 1024 * 1024


def shifted(x, axis, by):
    devices = lax.axis_size(axis)
    pairs = [(i, i + by) for i in range(devices) if 0 <= i + by < devices]
    return lax.ppermute(x, axis, pairs)


def from_behind(value, axis, steps):
    count = lax.axis_size(axis)
    pairs = [(source, (source + steps) % count) for source in range(count)]
    return lax.ppermute(value, axis, pairs)


def attend_kernel(start_ref, q_ref, kp_ref, ko_ref, vp_ref, vo_ref, out_ref, bias_ref):
    rows = q_ref.shape[0]
    tiles = rows // TILE
    keys_seen = PAGE + TILE

    @pl.when(pl.program_id(0) == 0)
    def _():
        for tile in range(tiles):
            shape = (TILE, keys_seen)
            query = lax.broadcasted_iota(jnp.int32, shape, 0) + tile * TILE
            key = lax.broadcasted_iota(jnp.int32, shape, 1) + (tile * TILE - PAGE)
            first = start_ref[tile * TILE : (tile + 1) * TILE, :]
            visible = (key >= first) & (key <= query)
            bias_ref[tile] = jnp.where(visible, 0.0, -1e30)

    for tile in range(tiles):
        lo = tile * TILE
        query = q_ref[lo : lo + TILE, :]
        parts_k = [kp_ref[lo:, :], ko_ref[: lo + TILE, :]]
        parts_v = [vp_ref[lo:, :], vo_ref[: lo + TILE, :]]
        key = jnp.concatenate(parts_k, 0)
        value = jnp.concatenate(parts_v, 0)
        scores = lax.dot_general(
            query, key, (((1,), (1,)), ((), ())), preferred_element_type=jnp.float32
        )
        scores = scores + bias_ref[tile]
        top = jnp.max(scores, axis=-1, keepdims=True)
        expo = jnp.exp2((scores - top) * (LOG2E / HD**0.5))
        total = jnp.sum(expo, axis=-1, keepdims=True)
        mixed = jnp.dot(expo.astype(jnp.bfloat16), value, preferred_element_type=jnp.float32)
        out_ref[lo : lo + TILE, :] = (mixed / total).astype(jnp.bfloat16)


def attend(queries, prev_kv, own_kv, start, first_head, heads, per_kv):
    rows = queries.shape[0]
    kv_spec = pl.BlockSpec((PAGE, HD), lambda h: (0, (first_head + h) // per_kv))
    return pl.pallas_call(
        attend_kernel,
        grid=(heads,),
        out_shape=jax.ShapeDtypeStruct((rows, heads * HD), jnp.bfloat16),
        in_specs=[
            pl.BlockSpec((rows, 1), lambda h: (0, 0)),
            pl.BlockSpec((rows, HD), lambda h: (0, first_head + h)),
            kv_spec,
            kv_spec,
            kv_spec,
            kv_spec,
        ],
        out_specs=pl.BlockSpec((rows, HD), lambda h: (0, h)),
        scratch_shapes=[pltpu.VMEM((rows // TILE, TILE, PAGE + TILE), jnp.float32)],
        compiler_params=pltpu.CompilerParams(vmem_limit_bytes=VMEM_LIMIT),
        cost_estimate=pl.CostEstimate(
            flops=heads * rows * (PAGE + TILE) * HD * 8,
            bytes_accessed=heads * rows * HD * 4,
            transcendentals=heads * rows * (PAGE + TILE),
        ),
    )(start, queries, prev_kv[0], own_kv[0], prev_kv[1], own_kv[1])


def gram_kernel(runs, widths, kinds, depth, rows, scale, has_acc, *refs):
    chunks = len(widths)
    offsets = [sum(widths[:c]) for c in range(chunks)]
    block = sum(widths)
    place_ref = refs[0]
    data = refs[1 : 1 + runs * kinds * chunks]
    rest = list(refs[1 + runs * kinds * chunks :])
    acc_ref = rest.pop(0) if has_acc else None
    out_ref = rest.pop(0)
    a_raw, a_t, b_buf, o_buf, a_sem, b_sem, o_sem = rest[:7]
    c_buf, c_sem = rest[7:] if has_acc else (None, None)

    def source(run, kind, chunk):
        return data[(run * kinds + kind) * chunks + chunk]

    tiles = [(k, c) for k in range(kinds) for c in range(chunks)]

    def b_copies(i):
        kind, chunk = tiles[i]
        slot = i % 2
        return [
            pltpu.make_async_copy(
                source(run, kind, chunk),
                b_buf.at[slot, pl.ds(run * depth, depth), pl.ds(0, widths[chunk])],
                b_sem.at[slot, run],
            )
            for run in range(runs)
        ]

    def columns(i):
        kind, chunk = tiles[i]
        return pl.ds(kind * block + offsets[chunk], widths[chunk])

    def c_copy(i):
        slot = i % 2
        return pltpu.make_async_copy(
            acc_ref.at[:, columns(i)],
            c_buf.at[slot, :, pl.ds(0, widths[tiles[i][1]])],
            c_sem.at[slot],
        )

    def o_copy(i):
        slot = i % 2
        return pltpu.make_async_copy(
            o_buf.at[slot, :, pl.ds(0, widths[tiles[i][1]])],
            out_ref.at[:, columns(i)],
            o_sem.at[slot],
        )

    def start(i):
        for copy in b_copies(i):
            copy.start()
        if has_acc:
            c_copy(i).start()

    place = place_ref[0]
    for where in range(block // rows):

        @pl.when(place == where)
        def _():
            lo, hi = where * rows, (where + 1) * rows
            copies = []
            for run in range(runs):
                piece = 0
                for chunk in range(chunks):
                    first = max(lo, offsets[chunk])
                    last = min(hi, offsets[chunk] + widths[chunk])
                    if first >= last:
                        continue
                    copies.append(
                        pltpu.make_async_copy(
                            source(run, 0, chunk).at[:, pl.ds(first - offsets[chunk], last - first)],
                            a_raw.at[pl.ds(run * depth, depth), pl.ds(first - lo, last - first)],
                            a_sem.at[run, piece],
                        )
                    )
                    piece += 1
            for copy in copies:
                copy.start()
            for copy in copies:
                copy.wait()

    start(0)
    a_t[...] = a_raw[...].T
    for i, (kind, chunk) in enumerate(tiles):
        slot = i % 2
        width = widths[chunk]
        if i + 1 < len(tiles):
            start(i + 1)
        for copy in b_copies(i):
            copy.wait()
        if i >= 2:
            o_copy(i - 2).wait()
        result = scale * jnp.dot(
            a_t[...], b_buf[slot, :, :width], preferred_element_type=jnp.float32
        )
        if has_acc:
            c_copy(i).wait()
            result = result + c_buf[slot, :, :width]
        o_buf[slot, :, :width] = result
        o_copy(i).start()
    for i in range(max(0, len(tiles) - 2), len(tiles)):
        o_copy(i).wait()


def gram(place, sources, rows, scale, acc=None):
    runs, kinds, chunks = len(sources), len(sources[0]), len(sources[0][0])
    widths = tuple(x.shape[1] for x in sources[0][0])
    depth = sources[0][0][0].shape[0]
    block = sum(widths)
    wide = max(widths)
    data = [x for run in sources for kind in run for x in kind]
    has_acc = acc is not None
    any_spec = pl.BlockSpec(memory_space=pl.ANY)
    operands = [place, *data] + ([acc] if has_acc else [])
    scratch = [
        pltpu.VMEM((runs * depth, rows), jnp.bfloat16),
        pltpu.VMEM((rows, runs * depth), jnp.bfloat16),
        pltpu.VMEM((2, runs * depth, wide), jnp.bfloat16),
        pltpu.VMEM((2, rows, wide), jnp.float32),
        pltpu.SemaphoreType.DMA((runs, chunks)),
        pltpu.SemaphoreType.DMA((2, runs)),
        pltpu.SemaphoreType.DMA((2,)),
    ]
    if has_acc:
        scratch += [pltpu.VMEM((2, rows, wide), jnp.float32), pltpu.SemaphoreType.DMA((2,))]
    return pl.pallas_call(
        functools.partial(gram_kernel, runs, widths, kinds, depth, rows, scale, has_acc),
        out_shape=jax.ShapeDtypeStruct((rows, kinds * block), jnp.float32),
        in_specs=[pl.BlockSpec(memory_space=pltpu.SMEM)] + [any_spec] * (len(operands) - 1),
        out_specs=any_spec,
        scratch_shapes=scratch,
        input_output_aliases={len(operands) - 1: 0} if has_acc else {},
        compiler_params=pltpu.CompilerParams(vmem_limit_bytes=VMEM_LIMIT),
        cost_estimate=pl.CostEstimate(
            flops=2 * runs * depth * rows * kinds * block,
            bytes_accessed=runs * depth * kinds * block * 2 + rows * kinds * block * (8 if has_acc else 4),
            transcendentals=0,
        ),
    )(*operands)


def own_kv_of(keys, values, local_heads):
    group = HEADS // KV_HEADS
    kv_count = max(1, local_heads // group)
    kv_first = lax.axis_index("tensor") * local_heads // group
    own_keys = lax.dynamic_slice_in_dim(keys, kv_first * HD, kv_count * HD, 1)
    own_values = lax.dynamic_slice_in_dim(values, kv_first * HD, kv_count * HD, 1)
    return (own_keys, own_values), kv_count


def per_device(queries, keys, values, page_start):
    tok_rows, slab_width = queries.shape
    local_heads = slab_width // HD
    runs = lax.axis_size("dp")
    own_kv, kv_count = own_kv_of(keys, values, local_heads)
    prev_kv = shifted(own_kv, "dp", 1)
    run_index = lax.axis_index("dp")
    start = (page_start - run_index * tok_rows).reshape(tok_rows, 1)
    per_kv = local_heads // kv_count

    size = local_heads // 6
    chunks = [(c * size, size) for c in range(6)]
    mirror_first = 1
    own = [[attend(queries, prev_kv, own_kv, start, h, n, per_kv)] for h, n in chunks]
    mirror = [[lax.ppermute(x[0], "tensor", [(t, t ^ 2) for t in range(4)])] for x in own]
    order = list(range(mirror_first, len(chunks))) + list(range(mirror_first))
    for _ in range(1, runs):
        for c in order:
            own[c].append(from_behind(own[c][-1], "dp", 1))
            if c < mirror_first:
                mirror[c].append(from_behind(mirror[c][-1], "dp", 1))
            else:
                mirror[c].append(lax.ppermute(own[c][-1], "tensor", [(t, t ^ 2) for t in range(4)]))
    even = lax.axis_index("tensor") % 2 == 0
    sibling = [
        [
            lax.ppermute(
                jnp.where(even, mirror[c][r], own[c][r]), "tensor", [(t, t ^ 1) for t in range(4)]
            )
            for r in range(runs)
        ]
        for c in range(len(chunks))
    ]

    def run_of(r):
        return [[x[r] for x in own], [x[r] for x in sibling], [x[r] for x in mirror]]

    rows = slab_width // runs
    scale = 2.0 / (tok_rows * runs)
    place = run_index.reshape(1)
    acc = gram(place, [run_of(r) for r in range(runs - 1)], rows, scale)
    return gram(place, [run_of(runs - 1)], rows, scale, acc)


def per_device_general(queries, keys, values, page_start):
    tok_rows, slab_width = queries.shape
    local_heads = slab_width // HD
    runs = lax.axis_size("dp")
    own_kv, kv_count = own_kv_of(keys, values, local_heads)
    prev_kv = shifted(own_kv, "dp", 1)
    run_index = lax.axis_index("dp")
    start = (page_start - run_index * tok_rows).reshape(tok_rows, 1)
    outputs = attend(queries, prev_kv, own_kv, start, 0, local_heads, local_heads // kv_count)
    steps = lax.axis_size("tensor") // 2 + 1
    rows = slab_width // runs
    moving = lax.all_gather(outputs, "dp", axis=0, tiled=True)
    left = lax.dynamic_slice_in_dim(moving, run_index * rows, rows, 1)
    tiles = []
    for offset in range(steps):
        if offset:
            moving = from_behind(moving, "tensor", -1)
        tiles.append(
            lax.dot_general(
                left, moving, (((0,), (0,)), ((), ())), preferred_element_type=jnp.float32
            )
        )
    return jnp.concatenate(tiles, 1) * (2.0 / (tok_rows * runs))


def solution(mesh):
    cores = mesh.shape["tensor"]
    rows = HEADS * HD // cores // mesh.shape["dp"]
    tuned = cores == 4 and rows % HD == 0
    return jax.shard_map(
        per_device if tuned else per_device_general,
        mesh=mesh,
        in_specs=(
            P(("groups", "dp"), "tensor"),
            P(("groups", "dp"), None),
            P(("groups", "dp"), None),
            P(("groups", "dp")),
        ),
        out_specs=P(("groups", "tensor", "dp"), None),
        check_vma=False,
    )
```

time: 1190 us -> 369 us (0.31)
  waiting for transfers between devices: 970 us -> 119 us
  starting transfers between devices: 8.84 us -> 137 us
  Pallas kernels: 0 us -> 95.6 us
  matrix products: 84.5 us -> 0 us
  other arithmetic: 79.4 us -> 11.4 us
  local copies, waits for them, and re-layouts: 34.9 us -> 4.01 us
  between operations: 13.5 us -> 1.08 us
    reduce_scatter x1 -> x0, waiting for transfers between devices: 923 us -> none  [per_device(): lax.psum_scatter(jnp.concatenate(tiles, 1).astype(jnp.bfloat16), 'dp', sc...]
    ppermute x0 -> x45, starting transfers between devices: none -> 121 us  [the longest x24 101 us: per_device(): lax.ppermute(jnp.where(even, mirror[c][r], own[c][r]), 'tensor', [(t, t ^...]
    pallas_call x0 -> x8, Pallas kernels: none -> 95.6 us  [the longest x2 57.1 us: gram(): pl.pallas_call(functools.partial(gram_kernel, runs, widths, kinds, depth,...]
    concatenate x3 -> x0, other arithmetic: 62.4 us -> none  [the longest x1 62.3 us: per_device(): jnp.concatenate(tiles, 1).astype(jnp.bfloat16)]
    dot_general x4 -> x0, matrix products: 58.4 us -> none  [the longest x3 41 us: per_device(): lax.dot_general(outputs, other, (((0,), (0,)), ((), ())), preferred_eleme...]
    ppermute x2 -> x21, waiting for transfers between devices: 46.9 us -> 85.8 us  [from_behind(): return lax.ppermute(value, axis, pairs)]
    ppermute x0 -> x45, waiting for transfers between devices: none -> 28.2 us  [the longest x15 22.8 us: per_device(): lax.ppermute(own[c][-1], 'tensor', [(t, t ^ 2) for t in range(4)])]
    mul x1 -> x0, local copies, waits for them, and re-layouts: 27.7 us -> none  [per_device(): return summed * (2.0 / total_tokens)]
  transfers between devices with their start and end apart: 5 -> 68, of which waited for: 4 -> 23; matrix products, arithmetic and copies ran while one was open for 3% -> 4% of each run, Pallas kernels for 0% -> 17%
where the time goes in v1:
time: 369 us; the launch traced here: 368 us
  starting transfers between devices  137 us (37%)
  waiting for transfers between devices  119 us (32%)
  Pallas kernels  95.6 us (26%)
  other arithmetic  11.4 us (3%)
  local copies, waits for them, and re-layouts  4.01 us (1%)
    ppermute x24, starting transfers between devices, per_device(): lax.ppermute(jnp.where(even, mirror[c][r], own[c][r]), 'tensor', [(t, t ^...  101 us
    ppermute x21, waiting for transfers between devices, from_behind(): return lax.ppermute(value, axis, pairs)  85.8 us
    pallas_call x2, Pallas kernels, gram(): pl.pallas_call(functools.partial(gram_kernel, runs, widths, kinds, depth,...  57.1 us
    pallas_call x6, Pallas kernels, attend(): pl.pallas_call(attend_kernel, grid=(heads,), out_shape=jax.ShapeDtypeStru...  38.5 us
    ppermute x15, waiting for transfers between devices, per_device(): lax.ppermute(own[c][-1], 'tensor', [(t, t ^ 2) for t in range(4)])  22.8 us
    ppermute x15, starting transfers between devices, per_device(): lax.ppermute(own[c][-1], 'tensor', [(t, t ^ 2) for t in range(4)])  15.6 us
    select_n x24, other arithmetic, per_device(): jnp.where(even, mirror[c][r], own[c][r])  10.7 us
    ppermute x21, starting transfers between devices, from_behind(): return lax.ppermute(value, axis, pairs)  8.02 us
  transfers between devices with their start and end apart: 68, of which 23 were waited for; matrix products, arithmetic and copies ran while one was open for 4% of the time, Pallas kernels for 17%

profile of v1, /device:TPU:1, one launch (start us, length us, event | category | flops | bytes accessed | tf_op | source)
XLA Modules:
  0.0 367.6 jit_solution(11509337135272552854)
XLA Ops:
  1.3 4.0 %collective-permute-start.1 = (bf16[512,256]{1,0:T(8,128)(2,1)S(1)}, bf16[512,256]{1,0:T(8,128)(2,1)S(1)}, u32[]{:S(2)}, u32[]{:S(2)}) collective-permute-start(bf16[512,256]{1,0:T(8,128)(2,1)S(1)} %constant_dynamic-slice_fusion.vo_ref), channel_id=1, source_target_pairs={{0,1},{1,2},{2,3},{4,5},{5,6},{6,7},{8,9},{9,10},{10,11},{12,13},{... | collective-permute-start | bytes 786440 | tf_op jit(solution)/shard_map/ppermute | solution.py:22
  6.3 3.2 collective-permute-start
  11.1 4.8 %collective-permute-done.kp_ref = bf16[512,256]{1,0:T(8,128)(2,1)S(1)} collective-permute-done((bf16[512,256]{1,0:T(8,128)(2,1)S(1)}, bf16[512,256]{1,0:T(8,128)(2,1)S(1)}, u32[]{:S(2)}, u32[]{:S(2)}) %collective-permute-start) | collective-permute-done | bytes 262176 | tf_op jit(solution)/shard_map/ppermute | solution.py:22
  16.6 6.4 %shard_map.46.refs_1_ = bf16[512,512]{1,0:T(8,128)(2,1)} custom-call(s32[512,1]{1,0:T(8,128)} %copy.6.start_ref, bf16[512,3072]{1,0:T(8,128)(2,1)} %q_ref.11, bf16[512,256]{1,0:T(8,128)(2,1)} %copy-done.57, bf16[512,256]{1,0:T(8,128)(2,1)} %copy-done.47, bf16[512,256]{1,0:T(8,128)(2,1)} %copy-done.56, bf16[512,256]{1,0:T(8,128)(2,1)} %copy-done.46), custom_call_target="tpu_custom_call" | custom-call | flops 1610612736 | bytes 1048576 | tf_op jit(solution)/shard_map/pallas_call | solution.py:67
  26.4 6.4 %shard_map.47.refs_2_ = bf16[512,512]{1,0:T(8,128)(2,1)} custom-call(s32[512,1]{1,0:T(8,128)} %copy.6.start_ref, bf16[512,3072]{1,0:T(8,128)(2,1)} %q_ref.11, bf16[512,256]{1,0:T(8,128)(2,1)} %copy-done.57, bf16[512,256]{1,0:T(8,128)(2,1)} %copy-done.47, bf16[512,256]{1,0:T(8,128)(2,1)} %copy-done.56, bf16[512,256]{1,0:T(8,128)(2,1)} %copy-done.46), custom_call_target="tpu_custom_call" | custom-call | flops 1610612736 | bytes 1048576 | tf_op jit(solution)/shard_map/pallas_call | solution.py:67
  34.4 6.4 %shard_map.48.refs_3_ = bf16[512,512]{1,0:T(8,128)(2,1)} custom-call(s32[512,1]{1,0:T(8,128)} %copy.6.start_ref, bf16[512,3072]{1,0:T(8,128)(2,1)} %q_ref.11, bf16[512,256]{1,0:T(8,128)(2,1)} %copy-done.57, bf16[512,256]{1,0:T(8,128)(2,1)} %copy-done.47, bf16[512,256]{1,0:T(8,128)(2,1)} %copy-done.56, bf16[512,256]{1,0:T(8,128)(2,1)} %copy-done.46), custom_call_target="tpu_custom_call" | custom-call | flops 1610612736 | bytes 1048576 | tf_op jit(solution)/shard_map/pallas_call | solution.py:67
  42.0 6.4 %shard_map.51.refs_6_ = bf16[512,512]{1,0:T(8,128)(2,1)} custom-call(s32[512,1]{1,0:T(8,128)} %copy.6.start_ref, bf16[512,3072]{1,0:T(8,128)(2,1)} %q_ref.11, bf16[512,256]{1,0:T(8,128)(2,1)} %copy-done.57, bf16[512,256]{1,0:T(8,128)(2,1)} %copy-done.47, bf16[512,256]{1,0:T(8,128)(2,1)} %copy-done.56, bf16[512,256]{1,0:T(8,128)(2,1)} %copy-done.46), custom_call_target="tpu_custom_call" | custom-call | flops 1610612736 | bytes 1048576 | tf_op jit(solution)/shard_map/pallas_call | solution.py:67
  48.4 6.4 %shard_map.50.refs_5_ = bf16[512,512]{1,0:T(8,128)(2,1)} custom-call(s32[512,1]{1,0:T(8,128)} %copy.6.start_ref, bf16[512,3072]{1,0:T(8,128)(2,1)} %q_ref.11, bf16[512,256]{1,0:T(8,128)(2,1)} %copy-done.57, bf16[512,256]{1,0:T(8,128)(2,1)} %copy-done.47, bf16[512,256]{1,0:T(8,128)(2,1)} %copy-done.56, bf16[512,256]{1,0:T(8,128)(2,1)} %copy-done.46), custom_call_target="tpu_custom_call" | custom-call | flops 1610612736 | bytes 1048576 | tf_op jit(solution)/shard_map/pallas_call | solution.py:67
  54.9 6.4 %shard_map.49.refs_4_ = bf16[512,512]{1,0:T(8,128)(2,1)} custom-call(s32[512,1]{1,0:T(8,128)} %copy.6.start_ref, bf16[512,3072]{1,0:T(8,128)(2,1)} %q_ref.11, bf16[512,256]{1,0:T(8,128)(2,1)} %copy-done.57, bf16[512,256]{1,0:T(8,128)(2,1)} %copy-done.47, bf16[512,256]{1,0:T(8,128)(2,1)} %copy-done.56, bf16[512,256]{1,0:T(8,128)(2,1)} %copy-done.46), custom_call_target="tpu_custom_call" | custom-call | flops 1610612736 | bytes 1048576 | tf_op jit(solution)/shard_map/pallas_call | solution.py:67
  66.7 5.4 %collective-permute-done.40.refs_16_ = bf16[512,512]{1,0:T(8,128)(2,1)S(1)} collective-permute-done((bf16[512,512]{1,0:T(8,128)(2,1)}, bf16[512,512]{1,0:T(8,128)(2,1)S(1)}, u32[]{:S(2)}, u32[]{:S(2)}) %collective-permute-start.40) | collective-permute-done | bytes 524320 | tf_op jit(solution)/shard_map/ppermute | solution.py:255
  75.9 9.3 %collective-permute-done.11.refs_22_ = bf16[512,512]{1,0:T(8,128)(2,1)S(1)} collective-permute-done((bf16[512,512]{1,0:T(8,128)(2,1)}, bf16[512,512]{1,0:T(8,128)(2,1)S(1)}, u32[]{:S(2)}, u32[]{:S(2)}) %collective-permute-start.11) | collective-permute-done | bytes 524320 | tf_op jit(solution)/shard_map/ppermute | solution.py:28
  85.2 7.9 %collective-permute-start.35 = (bf16[512,512]{1,0:T(8,128)(2,1)S(1)}, bf16[512,512]{1,0:T(8,128)(2,1)S(1)}, u32[]{:S(2)}, u32[]{:S(2)}) collective-permute-start(bf16[512,512]{1,0:T(8,128)(2,1)S(1)} %broadcast_select_fusion.17), channel_id=1, source_target_pairs={{0,4},{4,0},{8,12},{12,8},{1,5},{5,1},{9,13},{13,9},{2,6},{6,2},{1... | collective-permute-start | bytes 1572872 | tf_op jit(solution)/shard_map/ppermute | solution.py:267
  93.1 3.3 collective-permute-done.14.refs_23_
  99.9 7.7 %collective-permute-done.17.refs_24_ = bf16[512,512]{1,0:T(8,128)(2,1)S(1)} collective-permute-done((bf16[512,512]{1,0:T(8,128)(2,1)}, bf16[512,512]{1,0:T(8,128)(2,1)S(1)}, u32[]{:S(2)}, u32[]{:S(2)}) %collective-permute-start.17) | collective-permute-done | bytes 524320 | tf_op jit(solution)/shard_map/ppermute | solution.py:28
  107.6 7.9 %collective-permute-start.37 = (bf16[512,512]{1,0:T(8,128)(2,1)S(1)}, bf16[512,512]{1,0:T(8,128)(2,1)S(1)}, u32[]{:S(2)}, u32[]{:S(2)}) collective-permute-start(bf16[512,512]{1,0:T(8,128)(2,1)S(1)} %broadcast_select_fusion.16), channel_id=1, source_target_pairs={{0,4},{4,0},{8,12},{12,8},{1,5},{5,1},{9,13},{13,9},{2,6},{6,2},{1... | collective-permute-start | bytes 1572872 | tf_op jit(solution)/shard_map/ppermute | solution.py:267
  115.6 3.3 collective-permute-done.21.refs_31_
  118.9 11.2 %collective-permute-done.3.refs_37_ = bf16[512,512]{1,0:T(8,128)(2,1)S(1)} collective-permute-done((bf16[512,512]{1,0:T(8,128)(2,1)S(1)}, bf16[512,512]{1,0:T(8,128)(2,1)S(1)}, u32[]{:S(2)}, u32[]{:S(2)}) %collective-permute-start.3) | collective-permute-done | bytes 524320 | tf_op jit(solution)/shard_map/ppermute | solution.py:28
  131.7 8.5 %collective-permute-start.41 = (bf16[512,512]{1,0:T(8,128)(2,1)S(1)}, bf16[512,512]{1,0:T(8,128)(2,1)S(1)}, u32[]{:S(2)}, u32[]{:S(2)}) collective-permute-start(bf16[512,512]{1,0:T(8,128)(2,1)S(1)} %broadcast_select_fusion.14), channel_id=1, source_target_pairs={{0,4},{4,0},{8,12},{12,8},{1,5},{5,1},{9,13},{13,9},{2,6},{6,2},{1... | collective-permute-start | bytes 1572872 | tf_op jit(solution)/shard_map/ppermute | solution.py:267
  142.8 4.1 %collective-permute-done.51.refs_34_ = bf16[512,512]{1,0:T(8,128)(2,1)S(1)} collective-permute-done((bf16[512,512]{1,0:T(8,128)(2,1)S(1)}, bf16[512,512]{1,0:T(8,128)(2,1)S(1)}, u32[]{:S(2)}, u32[]{:S(2)}) %collective-permute-start.51) | collective-permute-done | bytes 524320 | tf_op jit(solution)/shard_map/ppermute | solution.py:263
  148.2 4.2 %collective-permute-done.9.refs_39_ = bf16[512,512]{1,0:T(8,128)(2,1)S(1)} collective-permute-done((bf16[512,512]{1,0:T(8,128)(2,1)S(1)}, bf16[512,512]{1,0:T(8,128)(2,1)S(1)}, u32[]{:S(2)}, u32[]{:S(2)}) %collective-permute-start.9) | collective-permute-done | bytes 524320 | tf_op jit(solution)/shard_map/ppermute | solution.py:28
  152.4 13.4 %collective-permute-start.43 = (bf16[512,512]{1,0:T(8,128)(2,1)S(1)}, bf16[512,512]{1,0:T(8,128)(2,1)S(1)}, u32[]{:S(2)}, u32[]{:S(2)}) collective-permute-start(bf16[512,512]{1,0:T(8,128)(2,1)S(1)} %broadcast_select_fusion.13), channel_id=1, source_target_pairs={{0,4},{4,0},{8,12},{12,8},{1,5},{5,1},{9,13},{13,9},{2,6},{6,2},{1... | collective-permute-start | bytes 1572872 | tf_op jit(solution)/shard_map/ppermute | solution.py:267
  166.0 3.3 collective-permute-done.55.refs_36_
  170.8 7.5 %collective-permute-done.15.refs_41_ = bf16[512,512]{1,0:T(8,128)(2,1)S(1)} collective-permute-done((bf16[512,512]{1,0:T(8,128)(2,1)S(1)}, bf16[512,512]{1,0:T(8,128)(2,1)S(1)}, u32[]{:S(2)}, u32[]{:S(2)}) %collective-permute-start.15) | collective-permute-done | bytes 524320 | tf_op jit(solution)/shard_map/ppermute | solution.py:28
  178.3 7.3 %collective-permute-start.46 = (bf16[512,512]{1,0:T(8,128)(2,1)S(1)}, bf16[512,512]{1,0:T(8,128)(2,1)S(1)}, u32[]{:S(2)}, u32[]{:S(2)}) collective-permute-start(bf16[512,512]{1,0:T(8,128)(2,1)S(1)} %broadcast_select_fusion.11), channel_id=1, source_target_pairs={{0,4},{4,0},{8,12},{12,8},{1,5},{5,1},{9,13},{13,9},{2,6},{6,2},{1... | collective-permute-start | bytes 1572872 | tf_op jit(solution)/shard_map/ppermute | solution.py:267
  185.7 3.9 %collective-permute-done.22.refs_49_ = bf16[512,512]{1,0:T(8,128)(2,1)S(1)} collective-permute-done((bf16[512,512]{1,0:T(8,128)(2,1)S(1)}, bf16[512,512]{1,0:T(8,128)(2,1)S(1)}, u32[]{:S(2)}, u32[]{:S(2)}) %collective-permute-start.22) | collective-permute-done | bytes 524320 | tf_op jit(solution)/shard_map/ppermute | solution.py:28
  191.3 9.6 %collective-permute-done.18.refs_42_ = bf16[512,512]{1,0:T(8,128)(2,1)S(1)} collective-permute-done((bf16[512,512]{1,0:T(8,128)(2,1)S(1)}, bf16[512,512]{1,0:T(8,128)(2,1)S(1)}, u32[]{:S(2)}, u32[]{:S(2)}) %collective-permute-start.18) | collective-permute-done | bytes 524320 | tf_op jit(solution)/shard_map/ppermute | solution.py:28
  200.8 7.0 %collective-permute-start.48 = (bf16[512,512]{1,0:T(8,128)(2,1)S(1)}, bf16[512,512]{1,0:T(8,128)(2,1)}, u32[]{:S(2)}, u32[]{:S(2)}) collective-permute-start(bf16[512,512]{1,0:T(8,128)(2,1)S(1)} %broadcast_select_fusion.10), channel_id=1, source_target_pairs={{0,4},{4,0},{8,12},{12,8},{1,5},{5,1},{9,13},{13,9},{2,6},{6,2},{1... | collective-permute-start | bytes 1572872 | tf_op jit(solution)/shard_map/ppermute | solution.py:267
  208.0 4.1 %collective-permute-done.4.refs_1_ = bf16[512,512]{1,0:T(8,128)(2,1)S(1)} collective-permute-done((bf16[512,512]{1,0:T(8,128)(2,1)S(1)}, bf16[512,512]{1,0:T(8,128)(2,1)S(1)}, u32[]{:S(2)}, u32[]{:S(2)}) %collective-permute-start.4) | collective-permute-done | bytes 524320 | tf_op jit(solution)/shard_map/ppermute | solution.py:28
  213.7 7.2 %collective-permute-start.50 = (bf16[512,512]{1,0:T(8,128)(2,1)S(1)}, bf16[512,512]{1,0:T(8,128)(2,1)S(1)}, u32[]{:S(2)}, u32[]{:S(2)}) collective-permute-start(bf16[512,512]{1,0:T(8,128)(2,1)S(1)} %broadcast_select_fusion.9), channel_id=1, source_target_pairs={{0,4},{4,0},{8,12},{12,8},{1,5},{5,1},{9,13},{13,9},{2,6},{6,2},{1... | collective-permute-start | bytes 1572872 | tf_op jit(solution)/shard_map/ppermute | solution.py:267
  221.0 2.8 collective-permute-done.7.refs_2_
  223.7 6.2 %collective-permute-start.52 = (bf16[512,512]{1,0:T(8,128)(2,1)S(1)}, bf16[512,512]{1,0:T(8,128)(2,1)}, u32[]{:S(2)}, u32[]{:S(2)}) collective-permute-start(bf16[512,512]{1,0:T(8,128)(2,1)S(1)} %broadcast_select_fusion.8), channel_id=1, source_target_pairs={{0,4},{4,0},{8,12},{12,8},{1,5},{5,1},{9,13},{13,9},{2,6},{6,2},{1... | collective-permute-start | bytes 1572872 | tf_op jit(solution)/shard_map/ppermute | solution.py:267
  229.9 5.1 %collective-permute-done.10.refs_3_ = bf16[512,512]{1,0:T(8,128)(2,1)S(1)} collective-permute-done((bf16[512,512]{1,0:T(8,128)(2,1)S(1)}, bf16[512,512]{1,0:T(8,128)(2,1)S(1)}, u32[]{:S(2)}, u32[]{:S(2)}) %collective-permute-start.10) | collective-permute-done | bytes 524320 | tf_op jit(solution)/shard_map/ppermute | solution.py:28
  236.7 3.9 %collective-permute-start.54 = (bf16[512,512]{1,0:T(8,128)(2,1)S(1)}, bf16[512,512]{1,0:T(8,128)(2,1)}, u32[]{:S(2)}, u32[]{:S(2)}) collective-permute-start(bf16[512,512]{1,0:T(8,128)(2,1)S(1)} %broadcast_select_fusion.7), channel_id=1, source_target_pairs={{0,4},{4,0},{8,12},{12,8},{1,5},{5,1},{9,13},{13,9},{2,6},{6,2},{1... | collective-permute-start | bytes 1572872 | tf_op jit(solution)/shard_map/ppermute | solution.py:267
  240.6 6.3 %collective-permute-done.13.refs_4_ = bf16[512,512]{1,0:T(8,128)(2,1)S(1)} collective-permute-done((bf16[512,512]{1,0:T(8,128)(2,1)S(1)}, bf16[512,512]{1,0:T(8,128)(2,1)S(1)}, u32[]{:S(2)}, u32[]{:S(2)}) %collective-permute-start.13) | collective-permute-done | bytes 524320 | tf_op jit(solution)/shard_map/ppermute | solution.py:28
  247.2 9.3 %collective-permute-done.27.refs_15_ = bf16[512,512]{1,0:T(8,128)(2,1)S(1)} collective-permute-done((bf16[512,512]{1,0:T(8,128)(2,1)S(1)}, bf16[512,512]{1,0:T(8,128)(2,1)S(1)}, u32[]{:S(2)}, u32[]{:S(2)}) %collective-permute-start.27) | collective-permute-done | bytes 524320 | tf_op jit(solution)/shard_map/ppermute | solution.py:263
  260.4 3.5 collective-permute-start.56
  263.9 2.2 collective-permute-start.57
  266.1 3.2 collective-permute-done.19.refs_6_
  269.4 8.0 %collective-permute-start.59 = (bf16[512,512]{1,0:T(8,128)(2,1)S(1)}, bf16[512,512]{1,0:T(8,128)(2,1)}, u32[]{:S(2)}, u32[]{:S(2)}) collective-permute-start(bf16[512,512]{1,0:T(8,128)(2,1)S(1)} %broadcast_select_fusion.4), channel_id=1, source_target_pairs={{0,4},{4,0},{8,12},{12,8},{1,5},{5,1},{9,13},{13,9},{2,6},{6,2},{1... | collective-permute-start | bytes 1572872 | tf_op jit(solution)/shard_map/ppermute | solution.py:267
  277.4 3.2 collective-permute-done.23.refs_13_
  280.6 2.2 collective-permute-start.31
  283.9 3.9 %collective-permute-start.61 = (bf16[512,512]{1,0:T(8,128)(2,1)S(1)}, bf16[512,512]{1,0:T(8,128)(2,1)}, u32[]{:S(2)}, u32[]{:S(2)}) collective-permute-start(bf16[512,512]{1,0:T(8,128)(2,1)S(1)} %broadcast_select_fusion.3), channel_id=1, source_target_pairs={{0,4},{4,0},{8,12},{12,8},{1,5},{5,1},{9,13},{13,9},{2,6},{6,2},{1... | collective-permute-start | bytes 1572872 | tf_op jit(solution)/shard_map/ppermute | solution.py:267
  288.4 3.0 collective-permute-done.31.refs_17_
  291.4 8.3 %collective-permute-start.67 = (bf16[512,512]{1,0:T(8,128)(2,1)S(1)}, bf16[512,512]{1,0:T(8,128)(2,1)}, u32[]{:S(2)}, u32[]{:S(2)}) collective-permute-start(bf16[512,512]{1,0:T(8,128)(2,1)S(1)} %broadcast_select_fusion), channel_id=1, source_target_pairs={{0,4},{4,0},{8,12},{12,8},{1,5},{5,1},{9,13},{13,9},{2,6},{6,2},{1... | collective-permute-start | bytes 1572872 | tf_op jit(solution)/shard_map/ppermute | solution.py:267
  299.7 2.9 collective-permute-done.33.refs_18_
  302.6 4.3 %collective-permute-start.24 = (bf16[512,512]{1,0:T(8,128)(2,1)S(1)}, bf16[512,512]{1,0:T(8,128)(2,1)S(1)}, u32[]{:S(2)}, u32[]{:S(2)}) collective-permute-start(bf16[512,512]{1,0:T(8,128)(2,1)S(1)} %broadcast_select_fusion.23), channel_id=1, source_target_pairs={{0,4},{4,0},{8,12},{12,8},{1,5},{5,1},{9,13},{13,9},{2,6},{6,2},{1... | collective-permute-start | bytes 1572872 | tf_op jit(solution)/shard_map/ppermute | solution.py:267
  310.1 29.7 %shard_map.52.refs_19_ = f32[768,9216]{1,0:T(8,128)} custom-call(s32[1]{0:T(128)} %bitcast.refs_0_, bf16[512,512]{1,0:T(8,128)(2,1)} %shard_map.46.refs_1_, bf16[512,512]{1,0:T(8,128)(2,1)} %shard_map.47.refs_2_, bf16[512,512]{1,0:T(8,128)(2,1)} %shard_map.48.refs_3_, bf16[512,512]{1,0:T(8,128)(2,1)} %shard_map.49.refs_4_, ...), custom_call_target="tpu_custom_call" | custom-call | flops 21743271936 | bytes 56623104 | tf_op jit(solution)/shard_map/pallas_call | solution.py:216
  340.0 27.4 %shard_map.53 = f32[768,9216]{1,0:T(8,128)} custom-call(s32[1]{0:T(128)} %bitcast.refs_0_, bf16[512,512]{1,0:T(8,128)(2,1)} %copy-done.2, bf16[512,512]{1,0:T(8,128)(2,1)} %copy-done.3, bf16[512,512]{1,0:T(8,128)(2,1)} %copy-done.4, bf16[512,512]{1,0:T(8,128)(2,1)} %copy-done.5, bf16[512,512]{1,0:T(8,128)(2,1)} %copy-done.8, ...), custom_call_target="tpu_custom_call", output_to_operand_aliasing={{}: (19, {})} | custom-call | flops 7247757312 | bytes 66060288 | tf_op jit(solution)/shard_map/pallas_call | solution.py:216
  (240 shorter events, 44.4 us)
Async XLA Ops:
  23.0 38.3 %collective-permute-start.20 = (bf16[512,512]{1,0:T(8,128)(2,1)}, bf16[512,512]{1,0:T(8,128)(2,1)S(1)}, u32[]{:S(2)}, u32[]{:S(2)}) collective-permute-start(bf16[512,512]{1,0:T(8,128)(2,1)} %shard_map.46.refs_1_), channel_id=1, source_target_pairs={{0,8},{4,12},{8,0},{12,4},{1,9},{5,13},{9,1},{13,5},{2,10},{6,14},... | collective-permute-start | bytes 1572872 | tf_op jit(solution)/shard_map/ppermute | solution.py:255
  24.2 39.9 %collective-permute-start.2 = (bf16[512,512]{1,0:T(8,128)(2,1)}, bf16[512,512]{1,0:T(8,128)(2,1)S(1)}, u32[]{:S(2)}, u32[]{:S(2)}) collective-permute-start(bf16[512,512]{1,0:T(8,128)(2,1)} %shard_map.46.refs_1_), channel_id=1, source_target_pairs={{0,1},{1,2},{2,3},{3,0},{4,5},{5,6},{6,7},{7,4},{8,9},{9,10},{10,1... | collective-permute-start | bytes 1572872 | tf_op jit(solution)/shard_map/ppermute | solution.py:28
  32.8 28.8 %collective-permute-start.36 = (bf16[512,512]{1,0:T(8,128)(2,1)}, bf16[512,512]{1,0:T(8,128)(2,1)S(1)}, u32[]{:S(2)}, u32[]{:S(2)}) collective-permute-start(bf16[512,512]{1,0:T(8,128)(2,1)} %shard_map.47.refs_2_), channel_id=1, source_target_pairs={{0,8},{4,12},{8,0},{12,4},{1,9},{5,13},{9,1},{13,5},{2,10},{6,14},... | collective-permute-start | bytes 1572872 | tf_op jit(solution)/shard_map/ppermute | solution.py:255
  33.1 31.3 %collective-permute-start.5 = (bf16[512,512]{1,0:T(8,128)(2,1)}, bf16[512,512]{1,0:T(8,128)(2,1)S(1)}, u32[]{:S(2)}, u32[]{:S(2)}) collective-permute-start(bf16[512,512]{1,0:T(8,128)(2,1)} %shard_map.47.refs_2_), channel_id=1, source_target_pairs={{0,1},{1,2},{2,3},{3,0},{4,5},{5,6},{6,7},{7,4},{8,9},{9,10},{10,1... | collective-permute-start | bytes 1572872 | tf_op jit(solution)/shard_map/ppermute | solution.py:28
  40.8 24.8 %collective-permute-start.38 = (bf16[512,512]{1,0:T(8,128)(2,1)}, bf16[512,512]{1,0:T(8,128)(2,1)S(1)}, u32[]{:S(2)}, u32[]{:S(2)}) collective-permute-start(bf16[512,512]{1,0:T(8,128)(2,1)} %shard_map.48.refs_3_), channel_id=1, source_target_pairs={{0,8},{4,12},{8,0},{12,4},{1,9},{5,13},{9,1},{13,5},{2,10},{6,14},... | collective-permute-start | bytes 1572872 | tf_op jit(solution)/shard_map/ppermute | solution.py:255
  64.1 21.0 %collective-permute-start.11 = (bf16[512,512]{1,0:T(8,128)(2,1)}, bf16[512,512]{1,0:T(8,128)(2,1)S(1)}, u32[]{:S(2)}, u32[]{:S(2)}) collective-permute-start(bf16[512,512]{1,0:T(8,128)(2,1)} %shard_map.49.refs_4_), channel_id=1, source_target_pairs={{0,1},{1,2},{2,3},{3,0},{4,5},{5,6},{6,7},{7,4},{8,9},{9,10},{10,1... | collective-permute-start | bytes 1572872 | tf_op jit(solution)/shard_map/ppermute | solution.py:28
  64.3 28.7 %collective-permute-start.42 = (bf16[512,512]{1,0:T(8,128)(2,1)}, bf16[512,512]{1,0:T(8,128)(2,1)S(1)}, u32[]{:S(2)}, u32[]{:S(2)}) collective-permute-start(bf16[512,512]{1,0:T(8,128)(2,1)} %shard_map.50.refs_5_), channel_id=1, source_target_pairs={{0,8},{4,12},{8,0},{12,4},{1,9},{5,13},{9,1},{13,5},{2,10},{6,14},... | collective-permute-start | bytes 1572872 | tf_op jit(solution)/shard_map/ppermute | solution.py:255
  65.6 30.8 %collective-permute-start.14 = (bf16[512,512]{1,0:T(8,128)(2,1)}, bf16[512,512]{1,0:T(8,128)(2,1)S(1)}, u32[]{:S(2)}, u32[]{:S(2)}) collective-permute-start(bf16[512,512]{1,0:T(8,128)(2,1)} %shard_map.50.refs_5_), channel_id=1, source_target_pairs={{0,1},{1,2},{2,3},{3,0},{4,5},{5,6},{6,7},{7,4},{8,9},{9,10},{10,1... | collective-permute-start | bytes 1572872 | tf_op jit(solution)/shard_map/ppermute | solution.py:28
  72.1 24.4 %collective-permute-start.44 = (bf16[512,512]{1,0:T(8,128)(2,1)}, bf16[512,512]{1,0:T(8,128)(2,1)S(1)}, u32[]{:S(2)}, u32[]{:S(2)}) collective-permute-start(bf16[512,512]{1,0:T(8,128)(2,1)} %shard_map.51.refs_6_), channel_id=1, source_target_pairs={{0,8},{4,12},{8,0},{12,4},{1,9},{5,13},{9,1},{13,5},{2,10},{6,14},... | collective-permute-start | bytes 1572872 | tf_op jit(solution)/shard_map/ppermute | solution.py:255
  74.5 33.1 %collective-permute-start.17 = (bf16[512,512]{1,0:T(8,128)(2,1)}, bf16[512,512]{1,0:T(8,128)(2,1)S(1)}, u32[]{:S(2)}, u32[]{:S(2)}) collective-permute-start(bf16[512,512]{1,0:T(8,128)(2,1)} %shard_map.51.refs_6_), channel_id=1, source_target_pairs={{0,1},{1,2},{2,3},{3,0},{4,5},{5,6},{6,7},{7,4},{8,9},{9,10},{10,1... | collective-permute-start | bytes 1572872 | tf_op jit(solution)/shard_map/ppermute | solution.py:28
  85.2 30.3 %collective-permute-start.35 = (bf16[512,512]{1,0:T(8,128)(2,1)S(1)}, bf16[512,512]{1,0:T(8,128)(2,1)S(1)}, u32[]{:S(2)}, u32[]{:S(2)}) collective-permute-start(bf16[512,512]{1,0:T(8,128)(2,1)S(1)} %broadcast_select_fusion.17), channel_id=1, source_target_pairs={{0,4},{4,0},{8,12},{12,8},{1,5},{5,1},{9,13},{13,9},{2,6},{6,2},{1... | collective-permute-start | bytes 1572872 | tf_op jit(solution)/shard_map/ppermute | solution.py:267
  93.1 25.8 %collective-permute-start.21 = (bf16[512,512]{1,0:T(8,128)(2,1)S(1)}, bf16[512,512]{1,0:T(8,128)(2,1)S(1)}, u32[]{:S(2)}, u32[]{:S(2)}) collective-permute-start(bf16[512,512]{1,0:T(8,128)(2,1)S(1)} %collective-permute-done.20.refs_13_), channel_id=1, source_target_pairs={{0,1},{1,2},{2,3},{3,0},{4,5},{5,6},{6,7},{7,4},{8,9},{9,10},{10,1... | collective-permute-start | bytes 1572872 | tf_op jit(solution)/shard_map/ppermute | solution.py:28
  96.4 33.7 %collective-permute-start.3 = (bf16[512,512]{1,0:T(8,128)(2,1)S(1)}, bf16[512,512]{1,0:T(8,128)(2,1)S(1)}, u32[]{:S(2)}, u32[]{:S(2)}) collective-permute-start(bf16[512,512]{1,0:T(8,128)(2,1)S(1)} %collective-permute-done.2.refs_19_), channel_id=1, source_target_pairs={{0,1},{1,2},{2,3},{3,0},{4,5},{5,6},{6,7},{7,4},{8,9},{9,10},{10,1... | collective-permute-start | bytes 1572872 | tf_op jit(solution)/shard_map/ppermute | solution.py:28
  96.4 34.9 %collective-permute-start.47 = (bf16[512,512]{1,0:T(8,128)(2,1)S(1)}, bf16[512,512]{1,0:T(8,128)(2,1)S(1)}, u32[]{:S(2)}, u32[]{:S(2)}) collective-permute-start(bf16[512,512]{1,0:T(8,128)(2,1)S(1)} %collective-permute-done.5.refs_20_), channel_id=1, source_target_pairs={{0,8},{4,12},{8,0},{12,4},{1,9},{5,13},{9,1},{13,5},{2,10},{6,14},... | collective-permute-start | bytes 1572872 | tf_op jit(solution)/shard_map/ppermute | solution.py:263
  107.6 24.1 %collective-permute-start.37 = (bf16[512,512]{1,0:T(8,128)(2,1)S(1)}, bf16[512,512]{1,0:T(8,128)(2,1)S(1)}, u32[]{:S(2)}, u32[]{:S(2)}) collective-permute-start(bf16[512,512]{1,0:T(8,128)(2,1)S(1)} %broadcast_select_fusion.16), channel_id=1, source_target_pairs={{0,4},{4,0},{8,12},{12,8},{1,5},{5,1},{9,13},{13,9},{2,6},{6,2},{1... | collective-permute-start | bytes 1572872 | tf_op jit(solution)/shard_map/ppermute | solution.py:267
  115.5 25.8 %collective-permute-start.39 = (bf16[512,512]{1,0:T(8,128)(2,1)S(1)}, bf16[512,512]{1,0:T(8,128)(2,1)S(1)}, u32[]{:S(2)}, u32[]{:S(2)}) collective-permute-start(bf16[512,512]{1,0:T(8,128)(2,1)S(1)} %broadcast_select_fusion.15), channel_id=1, source_target_pairs={{0,4},{4,0},{8,12},{12,8},{1,5},{5,1},{9,13},{13,9},{2,6},{6,2},{1... | collective-permute-start | bytes 1572872 | tf_op jit(solution)/shard_map/ppermute | solution.py:267
  118.9 22.5 %collective-permute-start.6 = (bf16[512,512]{1,0:T(8,128)(2,1)S(1)}, bf16[512,512]{1,0:T(8,128)(2,1)S(1)}, u32[]{:S(2)}, u32[]{:S(2)}) collective-permute-start(bf16[512,512]{1,0:T(8,128)(2,1)S(1)} %collective-permute-done.5.refs_20_), channel_id=1, source_target_pairs={{0,1},{1,2},{2,3},{3,0},{4,5},{5,6},{6,7},{7,4},{8,9},{9,10},{10,1... | collective-permute-start | bytes 1572872 | tf_op jit(solution)/shard_map/ppermute | solution.py:28
  131.7 34.1 %collective-permute-start.41 = (bf16[512,512]{1,0:T(8,128)(2,1)S(1)}, bf16[512,512]{1,0:T(8,128)(2,1)S(1)}, u32[]{:S(2)}, u32[]{:S(2)}) collective-permute-start(bf16[512,512]{1,0:T(8,128)(2,1)S(1)} %broadcast_select_fusion.14), channel_id=1, source_target_pairs={{0,4},{4,0},{8,12},{12,8},{1,5},{5,1},{9,13},{13,9},{2,6},{6,2},{1... | collective-permute-start | bytes 1572872 | tf_op jit(solution)/shard_map/ppermute | solution.py:267
  141.4 24.6 %collective-permute-start.12 = (bf16[512,512]{1,0:T(8,128)(2,1)S(1)}, bf16[512,512]{1,0:T(8,128)(2,1)S(1)}, u32[]{:S(2)}, u32[]{:S(2)}) collective-permute-start(bf16[512,512]{1,0:T(8,128)(2,1)S(1)} %collective-permute-done.11.refs_22_), channel_id=1, source_target_pairs={{0,1},{1,2},{2,3},{3,0},{4,5},{5,6},{6,7},{7,4},{8,9},{9,10},{10,1... | collective-permute-start | bytes 1572872 | tf_op jit(solution)/shard_map/ppermute | solution.py:28
  141.5 24.5 %collective-permute-start.53 = (bf16[512,512]{1,0:T(8,128)(2,1)S(1)}, bf16[512,512]{1,0:T(8,128)(2,1)S(1)}, u32[]{:S(2)}, u32[]{:S(2)}) collective-permute-start(bf16[512,512]{1,0:T(8,128)(2,1)S(1)} %collective-permute-done.14.refs_23_), channel_id=1, source_target_pairs={{0,8},{4,12},{8,0},{12,4},{1,9},{5,13},{9,1},{13,5},{2,10},{6,14},... | collective-permute-start | bytes 1572872 | tf_op jit(solution)/shard_map/ppermute | solution.py:263
  146.9 22.5 %collective-permute-start.55 = (bf16[512,512]{1,0:T(8,128)(2,1)S(1)}, bf16[512,512]{1,0:T(8,128)(2,1)S(1)}, u32[]{:S(2)}, u32[]{:S(2)}) collective-permute-start(bf16[512,512]{1,0:T(8,128)(2,1)S(1)} %collective-permute-done.17.refs_24_), channel_id=1, source_target_pairs={{0,8},{4,12},{8,0},{12,4},{1,9},{5,13},{9,1},{13,5},{2,10},{6,14},... | collective-permute-start | bytes 1572872 | tf_op jit(solution)/shard_map/ppermute | solution.py:263
  166.0 23.6 %collective-permute-start.22 = (bf16[512,512]{1,0:T(8,128)(2,1)S(1)}, bf16[512,512]{1,0:T(8,128)(2,1)S(1)}, u32[]{:S(2)}, u32[]{:S(2)}) collective-permute-start(bf16[512,512]{1,0:T(8,128)(2,1)S(1)} %collective-permute-done.21.refs_31_), channel_id=1, source_target_pairs={{0,1},{1,2},{2,3},{3,0},{4,5},{5,6},{6,7},{7,4},{8,9},{9,10},{10,1... | collective-permute-start | bytes 1572872 | tf_op jit(solution)/shard_map/ppermute | solution.py:28
  169.4 20.2 %collective-permute-start.58 = (bf16[512,512]{1,0:T(8,128)(2,1)S(1)}, bf16[512,512]{1,0:T(8,128)(2,1)S(1)}, u32[]{:S(2)}, u32[]{:S(2)}) collective-permute-start(bf16[512,512]{1,0:T(8,128)(2,1)S(1)} %collective-permute-done.6.refs_38_), channel_id=1, source_target_pairs={{0,8},{4,12},{8,0},{12,4},{1,9},{5,13},{9,1},{13,5},{2,10},{6,14},... | collective-permute-start | bytes 1572872 | tf_op jit(solution)/shard_map/ppermute | solution.py:263
  170.7 30.1 %collective-permute-start.18 = (bf16[512,512]{1,0:T(8,128)(2,1)S(1)}, bf16[512,512]{1,0:T(8,128)(2,1)S(1)}, u32[]{:S(2)}, u32[]{:S(2)}) collective-permute-start(bf16[512,512]{1,0:T(8,128)(2,1)S(1)} %collective-permute-done.17.refs_24_), channel_id=1, source_target_pairs={{0,1},{1,2},{2,3},{3,0},{4,5},{5,6},{6,7},{7,4},{8,9},{9,10},{10,1... | collective-permute-start | bytes 1572872 | tf_op jit(solution)/shard_map/ppermute | solution.py:28
  178.3 29.5 %collective-permute-start.46 = (bf16[512,512]{1,0:T(8,128)(2,1)S(1)}, bf16[512,512]{1,0:T(8,128)(2,1)S(1)}, u32[]{:S(2)}, u32[]{:S(2)}) collective-permute-start(bf16[512,512]{1,0:T(8,128)(2,1)S(1)} %broadcast_select_fusion.11), channel_id=1, source_target_pairs={{0,4},{4,0},{8,12},{12,8},{1,5},{5,1},{9,13},{13,9},{2,6},{6,2},{1... | collective-permute-start | bytes 1572872 | tf_op jit(solution)/shard_map/ppermute | solution.py:267
  185.6 26.4 %collective-permute-start.4 = (bf16[512,512]{1,0:T(8,128)(2,1)S(1)}, bf16[512,512]{1,0:T(8,128)(2,1)S(1)}, u32[]{:S(2)}, u32[]{:S(2)}) collective-permute-start(bf16[512,512]{1,0:T(8,128)(2,1)S(1)} %collective-permute-done.3.refs_37_), channel_id=1, source_target_pairs={{0,1},{1,2},{2,3},{3,0},{4,5},{5,6},{6,7},{7,4},{8,9},{9,10},{10,1... | collective-permute-start | bytes 1572872 | tf_op jit(solution)/shard_map/ppermute | solution.py:28
  189.6 22.5 %collective-permute-start.60 = (bf16[512,512]{1,0:T(8,128)(2,1)S(1)}, bf16[512,512]{1,0:T(8,128)(2,1)S(1)}, u32[]{:S(2)}, u32[]{:S(2)}) collective-permute-start(bf16[512,512]{1,0:T(8,128)(2,1)S(1)} %collective-permute-done.9.refs_39_), channel_id=1, source_target_pairs={{0,8},{4,12},{8,0},{12,4},{1,9},{5,13},{9,1},{13,5},{2,10},{6,14},... | collective-permute-start | bytes 1572872 | tf_op jit(solution)/shard_map/ppermute | solution.py:263
  189.6 22.5 %collective-permute-start.62 = (bf16[512,512]{1,0:T(8,128)(2,1)S(1)}, bf16[512,512]{1,0:T(8,128)(2,1)S(1)}, u32[]{:S(2)}, u32[]{:S(2)}) collective-permute-start(bf16[512,512]{1,0:T(8,128)(2,1)S(1)} %collective-permute-done.12.refs_40_), channel_id=1, source_target_pairs={{0,8},{4,12},{8,0},{12,4},{1,9},{5,13},{9,1},{13,5},{2,10},{6,14},... | collective-permute-start | bytes 1572872 | tf_op jit(solution)/shard_map/ppermute | solution.py:263
  212.0 22.9 %collective-permute-start.10 = (bf16[512,512]{1,0:T(8,128)(2,1)S(1)}, bf16[512,512]{1,0:T(8,128)(2,1)S(1)}, u32[]{:S(2)}, u32[]{:S(2)}) collective-permute-start(bf16[512,512]{1,0:T(8,128)(2,1)S(1)} %collective-permute-done.9.refs_39_), channel_id=1, source_target_pairs={{0,1},{1,2},{2,3},{3,0},{4,5},{5,6},{6,7},{7,4},{8,9},{9,10},{10,1... | collective-permute-start | bytes 1572872 | tf_op jit(solution)/shard_map/ppermute | solution.py:28
  212.1 22.9 %collective-permute-start.64 = (bf16[512,512]{1,0:T(8,128)(2,1)S(1)}, bf16[512,512]{1,0:T(8,128)(2,1)S(1)}, u32[]{:S(2)}, u32[]{:S(2)}) collective-permute-start(bf16[512,512]{1,0:T(8,128)(2,1)S(1)} %collective-permute-done.15.refs_41_), channel_id=1, source_target_pairs={{0,8},{4,12},{8,0},{12,4},{1,9},{5,13},{9,1},{13,5},{2,10},{6,14},... | collective-permute-start | bytes 1572872 | tf_op jit(solution)/shard_map/ppermute | solution.py:263
  212.2 24.1 %collective-permute-start.66 = (bf16[512,512]{1,0:T(8,128)(2,1)S(1)}, bf16[512,512]{1,0:T(8,128)(2,1)S(1)}, u32[]{:S(2)}, u32[]{:S(2)}) collective-permute-start(bf16[512,512]{1,0:T(8,128)(2,1)S(1)} %collective-permute-done.18.refs_42_), channel_id=1, source_target_pairs={{0,8},{4,12},{8,0},{12,4},{1,9},{5,13},{9,1},{13,5},{2,10},{6,14},... | collective-permute-start | bytes 1572872 | tf_op jit(solution)/shard_map/ppermute | solution.py:263
  213.7 23.0 %collective-permute-start.50 = (bf16[512,512]{1,0:T(8,128)(2,1)S(1)}, bf16[512,512]{1,0:T(8,128)(2,1)S(1)}, u32[]{:S(2)}, u32[]{:S(2)}) collective-permute-start(bf16[512,512]{1,0:T(8,128)(2,1)S(1)} %broadcast_select_fusion.9), channel_id=1, source_target_pairs={{0,4},{4,0},{8,12},{12,8},{1,5},{5,1},{9,13},{13,9},{2,6},{6,2},{1... | collective-permute-start | bytes 1572872 | tf_op jit(solution)/shard_map/ppermute | solution.py:267
  236.3 20.2 %collective-permute-start.27 = (bf16[512,512]{1,0:T(8,128)(2,1)S(1)}, bf16[512,512]{1,0:T(8,128)(2,1)S(1)}, u32[]{:S(2)}, u32[]{:S(2)}) collective-permute-start(bf16[512,512]{1,0:T(8,128)(2,1)S(1)} %collective-permute-done.10.refs_3_), channel_id=1, source_target_pairs={{0,8},{4,12},{8,0},{12,4},{1,9},{5,13},{9,1},{13,5},{2,10},{6,14},... | collective-permute-start | bytes 1572872 | tf_op jit(solution)/shard_map/ppermute | solution.py:263
  236.7 23.7 %collective-permute-start.54 = (bf16[512,512]{1,0:T(8,128)(2,1)S(1)}, bf16[512,512]{1,0:T(8,128)(2,1)}, u32[]{:S(2)}, u32[]{:S(2)}) collective-permute-start(bf16[512,512]{1,0:T(8,128)(2,1)S(1)} %broadcast_select_fusion.7), channel_id=1, source_target_pairs={{0,4},{4,0},{8,12},{12,8},{1,5},{5,1},{9,13},{13,9},{2,6},{6,2},{1... | collective-permute-start | bytes 1572872 | tf_op jit(solution)/shard_map/ppermute | solution.py:267
  240.6 23.3 %collective-permute-start.16 = (bf16[512,512]{1,0:T(8,128)(2,1)S(1)}, bf16[512,512]{1,0:T(8,128)(2,1)S(1)}, u32[]{:S(2)}, u32[]{:S(2)}) collective-permute-start(bf16[512,512]{1,0:T(8,128)(2,1)S(1)} %collective-permute-done.15.refs_41_), channel_id=1, source_target_pairs={{0,1},{1,2},{2,3},{3,0},{4,5},{5,6},{6,7},{7,4},{8,9},{9,10},{10,1... | collective-permute-start | bytes 1572872 | tf_op jit(solution)/shard_map/ppermute | solution.py:28
  246.9 22.5 %collective-permute-start.19 = (bf16[512,512]{1,0:T(8,128)(2,1)S(1)}, bf16[512,512]{1,0:T(8,128)(2,1)S(1)}, u32[]{:S(2)}, u32[]{:S(2)}) collective-permute-start(bf16[512,512]{1,0:T(8,128)(2,1)S(1)} %collective-permute-done.18.refs_42_), channel_id=1, source_target_pairs={{0,1},{1,2},{2,3},{3,0},{4,5},{5,6},{6,7},{7,4},{8,9},{9,10},{10,1... | collective-permute-start | bytes 1572872 | tf_op jit(solution)/shard_map/ppermute | solution.py:28
  246.9 33.7 %collective-permute-start.23 = (bf16[512,512]{1,0:T(8,128)(2,1)S(1)}, bf16[512,512]{1,0:T(8,128)(2,1)S(1)}, u32[]{:S(2)}, u32[]{:S(2)}) collective-permute-start(bf16[512,512]{1,0:T(8,128)(2,1)S(1)} %collective-permute-done.22.refs_49_), channel_id=1, source_target_pairs={{0,1},{1,2},{2,3},{3,0},{4,5},{5,6},{6,7},{7,4},{8,9},{9,10},{10,1... | collective-permute-start | bytes 1572872 | tf_op jit(solution)/shard_map/ppermute | solution.py:28
  256.5 26.4 %collective-permute-start.29 = (bf16[512,512]{1,0:T(8,128)(2,1)S(1)}, bf16[512,512]{1,0:T(8,128)(2,1)S(1)}, u32[]{:S(2)}, u32[]{:S(2)}) collective-permute-start(bf16[512,512]{1,0:T(8,128)(2,1)S(1)} %collective-permute-done.13.refs_4_), channel_id=1, source_target_pairs={{0,8},{4,12},{8,0},{12,4},{1,9},{5,13},{9,1},{13,5},{2,10},{6,14},... | collective-permute-start | bytes 1572872 | tf_op jit(solution)/shard_map/ppermute | solution.py:263
  260.4 23.5 %collective-permute-start.56 = (bf16[512,512]{1,0:T(8,128)(2,1)S(1)}, bf16[512,512]{1,0:T(8,128)(2,1)}, u32[]{:S(2)}, u32[]{:S(2)}) collective-permute-start(bf16[512,512]{1,0:T(8,128)(2,1)S(1)} %broadcast_select_fusion.6), channel_id=1, source_target_pairs={{0,4},{4,0},{8,12},{12,8},{1,5},{5,1},{9,13},{13,9},{2,6},{6,2},{1... | collective-permute-start | bytes 1572872 | tf_op jit(solution)/shard_map/ppermute | solution.py:267
  263.9 23.9 %collective-permute-start.57 = (bf16[512,512]{1,0:T(8,128)(2,1)S(1)}, bf16[512,512]{1,0:T(8,128)(2,1)}, u32[]{:S(2)}, u32[]{:S(2)}) collective-permute-start(bf16[512,512]{1,0:T(8,128)(2,1)S(1)} %broadcast_select_fusion.5), channel_id=1, source_target_pairs={{0,4},{4,0},{8,12},{12,8},{1,5},{5,1},{9,13},{13,9},{2,6},{6,2},{1... | collective-permute-start | bytes 1572872 | tf_op jit(solution)/shard_map/ppermute | solution.py:267
  283.9 24.7 %collective-permute-start.61 = (bf16[512,512]{1,0:T(8,128)(2,1)S(1)}, bf16[512,512]{1,0:T(8,128)(2,1)}, u32[]{:S(2)}, u32[]{:S(2)}) collective-permute-start(bf16[512,512]{1,0:T(8,128)(2,1)S(1)} %broadcast_select_fusion.3), channel_id=1, source_target_pairs={{0,4},{4,0},{8,12},{12,8},{1,5},{5,1},{9,13},{13,9},{2,6},{6,2},{1... | collective-permute-start | bytes 1572872 | tf_op jit(solution)/shard_map/ppermute | solution.py:267
  287.9 20.9 %collective-permute-start.63 = (bf16[512,512]{1,0:T(8,128)(2,1)S(1)}, bf16[512,512]{1,0:T(8,128)(2,1)}, u32[]{:S(2)}, u32[]{:S(2)}) collective-permute-start(bf16[512,512]{1,0:T(8,128)(2,1)S(1)} %broadcast_select_fusion.2), channel_id=1, source_target_pairs={{0,4},{4,0},{8,12},{12,8},{1,5},{5,1},{9,13},{13,9},{2,6},{6,2},{1... | collective-permute-start | bytes 1572872 | tf_op jit(solution)/shard_map/ppermute | solution.py:267
  287.9 21.3 %collective-permute-start.65 = (bf16[512,512]{1,0:T(8,128)(2,1)S(1)}, bf16[512,512]{1,0:T(8,128)(2,1)}, u32[]{:S(2)}, u32[]{:S(2)}) collective-permute-start(bf16[512,512]{1,0:T(8,128)(2,1)S(1)} %broadcast_select_fusion.1), channel_id=1, source_target_pairs={{0,4},{4,0},{8,12},{12,8},{1,5},{5,1},{9,13},{13,9},{2,6},{6,2},{1... | collective-permute-start | bytes 1572872 | tf_op jit(solution)/shard_map/ppermute | solution.py:267
  308.7 31.2 %collective-permute-start.26 = (bf16[512,512]{1,0:T(8,128)(2,1)}, bf16[512,512]{1,0:T(8,128)(2,1)}, u32[]{:S(2)}, u32[]{:S(2)}) collective-permute-start(bf16[512,512]{1,0:T(8,128)(2,1)} %broadcast_select_fusion.22), channel_id=1, source_target_pairs={{0,4},{4,0},{8,12},{12,8},{1,5},{5,1},{9,13},{13,9},{2,6},{6,2},{1... | collective-permute-start | bytes 1572872 | tf_op jit(solution)/shard_map/ppermute | solution.py:267
  308.8 31.1 %collective-permute-start.28 = (bf16[512,512]{1,0:T(8,128)(2,1)}, bf16[512,512]{1,0:T(8,128)(2,1)}, u32[]{:S(2)}, u32[]{:S(2)}) collective-permute-start(bf16[512,512]{1,0:T(8,128)(2,1)} %broadcast_select_fusion.21), channel_id=1, source_target_pairs={{0,4},{4,0},{8,12},{12,8},{1,5},{5,1},{9,13},{13,9},{2,6},{6,2},{1... | collective-permute-start | bytes 1572872 | tf_op jit(solution)/shard_map/ppermute | solution.py:267
  309.2 30.7 %collective-permute-start.30 = (bf16[512,512]{1,0:T(8,128)(2,1)}, bf16[512,512]{1,0:T(8,128)(2,1)}, u32[]{:S(2)}, u32[]{:S(2)}) collective-permute-start(bf16[512,512]{1,0:T(8,128)(2,1)} %broadcast_select_fusion.20), channel_id=1, source_target_pairs={{0,4},{4,0},{8,12},{12,8},{1,5},{5,1},{9,13},{13,9},{2,6},{6,2},{1... | collective-permute-start | bytes 1572872 | tf_op jit(solution)/shard_map/ppermute | solution.py:267
  309.3 30.6 %collective-permute-start.32 = (bf16[512,512]{1,0:T(8,128)(2,1)}, bf16[512,512]{1,0:T(8,128)(2,1)}, u32[]{:S(2)}, u32[]{:S(2)}) collective-permute-start(bf16[512,512]{1,0:T(8,128)(2,1)} %broadcast_select_fusion.19), channel_id=1, source_target_pairs={{0,4},{4,0},{8,12},{12,8},{1,5},{5,1},{9,13},{13,9},{2,6},{6,2},{1... | collective-permute-start | bytes 1572872 | tf_op jit(solution)/shard_map/ppermute | solution.py:267
  309.7 30.2 %collective-permute-start.34 = (bf16[512,512]{1,0:T(8,128)(2,1)}, bf16[512,512]{1,0:T(8,128)(2,1)}, u32[]{:S(2)}, u32[]{:S(2)}) collective-permute-start(bf16[512,512]{1,0:T(8,128)(2,1)} %broadcast_select_fusion.18), channel_id=1, source_target_pairs={{0,4},{4,0},{8,12},{12,8},{1,5},{5,1},{9,13},{13,9},{2,6},{6,2},{1... | collective-permute-start | bytes 1572872 | tf_op jit(solution)/shard_map/ppermute | solution.py:267
  (78 other events, 6458.2 us)

commit v2 on v0

v2 whole, which is shorter than its diff:
```python
import functools

import jax
import jax.numpy as jnp
from jax import lax
from jax.experimental import pallas as pl
from jax.experimental.pallas import tpu as pltpu
from jax.sharding import PartitionSpec as P

HEADS = 96
HD = 128
KV_HEADS = 8
PAGE = 512
TILE = 256
LOG2E = 1.4426950408889634
VMEM_LIMIT = 56 * 1024 * 1024


def shifted(x, axis, by):
    devices = lax.axis_size(axis)
    pairs = [(i, i + by) for i in range(devices) if 0 <= i + by < devices]
    return lax.ppermute(x, axis, pairs)


def from_behind(value, axis, steps):
    count = lax.axis_size(axis)
    pairs = [(source, (source + steps) % count) for source in range(count)]
    return lax.ppermute(value, axis, pairs)


def over_tensor(value, bit):
    count = lax.axis_size("tensor")
    return lax.ppermute(value, "tensor", [(t, t ^ bit) for t in range(count)])


def tie(value, *after):
    return lax.optimization_barrier((value, *after))[0] if after else value


def held(value, out, *after):
    if out is None:
        return tie(value, *after), None
    return lax.optimization_barrier((value, out, *after))[:2]


def attend_kernel(start_ref, q_ref, kp_ref, ko_ref, vp_ref, vo_ref, out_ref, bias_ref):
    rows = q_ref.shape[0]
    tiles = rows // TILE
    keys_seen = PAGE + TILE

    @pl.when(pl.program_id(0) == 0)
    def _():
        for tile in range(tiles):
            shape = (TILE, keys_seen)
            query = lax.broadcasted_iota(jnp.int32, shape, 0) + tile * TILE
            key = lax.broadcasted_iota(jnp.int32, shape, 1) + (tile * TILE - PAGE)
            first = start_ref[tile * TILE : (tile + 1) * TILE, :]
            visible = (key >= first) & (key <= query)
            bias_ref[tile] = jnp.where(visible, 0.0, -1e30)

    for tile in range(tiles):
        lo = tile * TILE
        query = q_ref[lo : lo + TILE, :]
        parts_k = [kp_ref[lo:, :], ko_ref[: lo + TILE, :]]
        parts_v = [vp_ref[lo:, :], vo_ref[: lo + TILE, :]]
        key = jnp.concatenate(parts_k, 0)
        value = jnp.concatenate(parts_v, 0)
        scores = lax.dot_general(
            query, key, (((1,), (1,)), ((), ())), preferred_element_type=jnp.float32
        )
        scores = scores + bias_ref[tile]
        top = jnp.max(scores, axis=-1, keepdims=True)
        expo = jnp.exp2((scores - top) * (LOG2E / HD**0.5))
        total = jnp.sum(expo, axis=-1, keepdims=True)
        mixed = jnp.dot(expo.astype(jnp.bfloat16), value, preferred_element_type=jnp.float32)
        out_ref[lo : lo + TILE, :] = (mixed / total).astype(jnp.bfloat16)


def attend(queries, own_kv, prev_kv, start, first_head, heads):
    rows = queries.shape[0]
    key_spec = pl.BlockSpec((PAGE, HD), lambda h: (0, 0))
    value_spec = pl.BlockSpec((PAGE, HD), lambda h: (0, 1))
    return pl.pallas_call(
        attend_kernel,
        grid=(heads,),
        out_shape=jax.ShapeDtypeStruct((rows, heads * HD), jnp.bfloat16),
        in_specs=[
            pl.BlockSpec((rows, 1), lambda h: (0, 0)),
            pl.BlockSpec((rows, HD), lambda h: (0, first_head + h)),
            key_spec,
            key_spec,
            value_spec,
            value_spec,
        ],
        out_specs=pl.BlockSpec((rows, HD), lambda h: (0, h)),
        scratch_shapes=[pltpu.VMEM((rows // TILE, TILE, PAGE + TILE), jnp.float32)],
        compiler_params=pltpu.CompilerParams(vmem_limit_bytes=VMEM_LIMIT),
        cost_estimate=pl.CostEstimate(flops=10**15, bytes_accessed=1, transcendentals=0),
    )(start, queries, prev_kv, own_kv, prev_kv, own_kv)


def rows_kernel(widths, rows, place_ref, *refs):
    chunks = len(widths)
    sources, (out_ref, raw, sem) = refs[:chunks], refs[chunks:]
    offsets = [sum(widths[:c]) for c in range(chunks)]
    for where in range(sum(widths) // rows):

        @pl.when(place_ref[0] == where)
        def _():
            lo, hi = where * rows, (where + 1) * rows
            copies = []
            for c in range(chunks):
                first, last = max(lo, offsets[c]), min(hi, offsets[c] + widths[c])
                if first < last:
                    copies.append(
                        pltpu.make_async_copy(
                            sources[c].at[:, pl.ds(first - offsets[c], last - first)],
                            raw.at[:, pl.ds(first - lo, last - first)],
                            sem.at[len(copies)],
                        )
                    )
            for copy in copies:
                copy.start()
            for copy in copies:
                copy.wait()

    out_ref[...] = raw[...].T


def rows_of(place, pieces, rows):
    depth = pieces[0].shape[0]
    widths = tuple(x.shape[1] for x in pieces)
    return pl.pallas_call(
        functools.partial(rows_kernel, widths, rows),
        out_shape=jax.ShapeDtypeStruct((rows, depth), jnp.bfloat16),
        in_specs=[pl.BlockSpec(memory_space=pltpu.SMEM)]
        + [pl.BlockSpec(memory_space=pltpu.HBM)] * len(pieces),
        scratch_shapes=[
            pltpu.VMEM((depth, rows), jnp.bfloat16),
            pltpu.SemaphoreType.DMA((len(pieces),)),
        ],
        compiler_params=pltpu.CompilerParams(vmem_limit_bytes=VMEM_LIMIT),
        cost_estimate=pl.CostEstimate(flops=10**15, bytes_accessed=1, transcendentals=0),
    )(place, *pieces)


def gram_kernel(runs, tiles, starts, depth, scale, kept, added, *refs):
    lefts, refs = refs[:runs], refs[runs:]
    data, refs = refs[: runs * len(tiles)], list(refs[runs * len(tiles) :])
    old_ref = refs.pop(0) if kept else None
    out_ref, left, b_buf, o_buf, left_sem, b_sem, o_sem = refs[:7]
    c_buf, c_sem = refs[7:] if added else (None, None)
    slots = b_buf.shape[0]

    def in_copies(i):
        slot = i % slots
        width = tiles[i][1]
        copies = [
            pltpu.make_async_copy(
                data[i * runs + run].at[:, pl.ds(starts[i * runs + run], width)],
                b_buf.at[slot, pl.ds(run * depth, depth), pl.ds(0, width)],
                b_sem.at[slot, run],
            )
            for run in range(runs)
        ]
        if added:
            copies.append(
                pltpu.make_async_copy(
                    old_ref.at[:, pl.ds(*tiles[i])],
                    c_buf.at[slot, :, pl.ds(0, width)],
                    c_sem.at[slot],
                )
            )
        return copies

    def out_copy(i):
        slot = i % slots
        return pltpu.make_async_copy(
            o_buf.at[slot, :, pl.ds(0, tiles[i][1])],
            out_ref.at[:, pl.ds(*tiles[i])],
            o_sem.at[slot],
        )

    left_copies = [
        pltpu.make_async_copy(
            lefts[run], left.at[:, pl.ds(run * depth, depth)], left_sem.at[run]
        )
        for run in range(runs)
    ]
    for copy in left_copies + in_copies(0):
        copy.start()
    for copy in left_copies:
        copy.wait()
    for i in range(1, min(slots - 1, len(tiles))):
        for copy in in_copies(i):
            copy.start()
    for i, (_, width) in enumerate(tiles):
        slot = i % slots
        if i + slots - 1 < len(tiles):
            for copy in in_copies(i + slots - 1):
                copy.start()
        for copy in in_copies(i):
            copy.wait()
        if i >= slots:
            out_copy(i - slots).wait()
        result = scale * jnp.dot(
            left[...], b_buf[slot, :, :width], preferred_element_type=jnp.float32
        )
        if added:
            result = result + c_buf[slot, :, :width]
        o_buf[slot, :, :width] = result
        out_copy(i).start()
    for i in range(max(0, len(tiles) - slots), len(tiles)):
        out_copy(i).wait()


def gram(out, lefts, tiles, width, columns, scale, added=False):
    runs = len(lefts)
    rows, depth = lefts[0].shape
    places = [(first, width) for first, _ in tiles]
    data = [x for _, arrays in tiles for x, _ in arrays]
    starts = [x for _, arrays in tiles for _, x in arrays]
    kept = out is not None
    any_spec = pl.BlockSpec(memory_space=pltpu.HBM)
    operands = [*lefts, *data] + ([out] if kept else [])
    slots = min(4, len(tiles))
    scratch = [
        pltpu.VMEM((rows, runs * depth), jnp.bfloat16),
        pltpu.VMEM((slots, runs * depth, width), jnp.bfloat16),
        pltpu.VMEM((slots, rows, width), jnp.float32),
        pltpu.SemaphoreType.DMA((runs,)),
        pltpu.SemaphoreType.DMA((slots, runs)),
        pltpu.SemaphoreType.DMA((slots,)),
    ]
    if added:
        scratch += [pltpu.VMEM((slots, rows, width), jnp.float32), pltpu.SemaphoreType.DMA((slots,))]
    total = sum(width for _, width in places)
    return pl.pallas_call(
        functools.partial(gram_kernel, runs, places, starts, depth, scale, kept, added),
        out_shape=jax.ShapeDtypeStruct((rows, columns), jnp.float32),
        in_specs=[any_spec] * len(operands),
        out_specs=any_spec,
        scratch_shapes=scratch,
        input_output_aliases={len(operands) - 1: 0} if kept else {},
        compiler_params=pltpu.CompilerParams(vmem_limit_bytes=VMEM_LIMIT),
        cost_estimate=pl.CostEstimate(flops=10**15, bytes_accessed=1, transcendentals=0),
    )(*operands)


def kv_of(keys, values, local_heads):
    group = HEADS // KV_HEADS
    kv_count = max(1, local_heads // group)
    kv_first = lax.axis_index("tensor") * local_heads // group
    own, prev = [], []
    for k in range(kv_count):
        parts = [lax.dynamic_slice_in_dim(x, (kv_first + k) * HD, HD, 1) for x in (keys, values)]
        own.append(jnp.concatenate(parts, 1))
        prev.append(shifted(own[k], "dp", 1))
    return list(zip(own, prev)), local_heads // kv_count


CHUNKS = 6


def per_device(queries, keys, values, page_start):
    tok_rows, slab = queries.shape
    local_heads = slab // HD
    runs = lax.axis_size("dp")
    kv, per_kv = kv_of(keys, values, local_heads)
    run_index = lax.axis_index("dp")
    start = (page_start - run_index * tok_rows).reshape(tok_rows, 1)
    place = run_index.reshape(1)
    rows = slab // runs
    scale = 2.0 / (tok_rows * runs)
    even = lax.axis_index("tensor") % 2 == 0

    size = local_heads // CHUNKS
    width = size * HD
    own, mirror, sibling = {}, {}, {}
    within = {}
    half = CHUNKS // 2
    last = runs - 1
    over_z = [("own", c, r) for r in range(1, runs) for c in range(CHUNKS)]
    over_z += [("mirror", c, last) for c in range(half, CHUNKS)]
    over_y = [(c, r) for r in range(last) for c in range(CHUNKS)]
    over_y += [(c, last) for c in range(half)]

    left = {}
    out = None
    steps = max(len(over_z), len(over_y))
    ended = {}
    swapped = []
    def tiles(kinds, chosen, some_runs):
        tables = (own, sibling, mirror)
        return [
            (
                k * slab + c * width,
                [(tables[k][c, r], within[c, r] if k == 1 else 0) for r in some_runs],
            )
            for c in chosen
            for k in kinds
        ]

    def rows_for(some_runs):
        for r in some_runs:
            if r not in left:
                left[r] = rows_of(place, [own[c, r] for c in range(CHUNKS)], rows)
        return [left[r] for r in some_runs]

    every = list(range(runs))
    everything = list(range(CHUNKS))
    first_runs, last_runs = every[: runs // 2], every[runs // 2 :]
    moved = (2, 1)
    done = last * CHUNKS
    work = {
        done - 12: [("rows", 0)],
        done - 11: [("rows", 1)],
        done - 10: [((0,), everything, first_runs, False)],
        done - 8: [(moved, [0, 1], first_runs, False)],
        done - 6: [(moved, [2, 3], first_runs, False)],
        done - 4: [(moved, [4, 5], first_runs, False)],
        done - 2: [("rows", 2)],
        done + 1: [("rows", 3)],
        done + 2: [((0,), everything, last_runs, True)],
        done + 3: [(moved, [0, half], last_runs, True)],
        done + 4: [(moved, [1, half + 1], last_runs, True)],
        done + 5: [(moved, [half - 1, CHUNKS - 1], last_runs, True)],
    }

    for step in range(steps + 3):
        before = ended.get(step - 2, [])
        if step < CHUNKS:
            first = step * size
            some = tie(start, *[prev for _, prev in kv]) if step == 1 else start
            own[step, 0] = attend(queries, *kv[first // per_kv], some, first, size)
        arrived = []
        if step < len(over_z):
            kind, c, r = over_z[step]
            table = own if kind == "own" else mirror
            value, out = held(table[c, r - 1], out, *before)
            table[c, r] = from_behind(value, "dp", 1)
            arrived.append(table[c, r])
        if step < len(over_y):
            c, r = over_y[step]
            value, out = held(own[c, r], out, *before)
            mirror[c, r] = over_tensor(value, 2)
            arrived.append(mirror[c, r])
        ended[step] = arrived
        past = step - 2
        swaps = over_y[past : past + 1] if past >= 0 else []
        swaps = swaps + [x[1:] for x in over_z[max(past, 0) : max(past + 1, 0)] if x[0] == "mirror"]
        if swaps:
            pair = ([mirror[x] for x in swaps], [own[x] for x in swaps])
            pair, out = held(pair, out, *before, *swapped)
            sent = jnp.where(even, *[jnp.concatenate(x, 1) for x in pair])
            sent = over_tensor(sent, 1)
            swapped = [sent]
            sibling.update({x: sent for x in swaps})
            within.update({x: i * width for i, x in enumerate(swaps)})
        for job in work.pop(step, ()):
            if job[0] == "rows":
                ended[step] += rows_for([job[1]])
            else:
                kinds, chosen, some_runs, added = job
                lefts, pieces = rows_for(some_runs), tiles(kinds, chosen, some_runs)
                out = gram(out, lefts, pieces, width, 3 * slab, scale, added)
    assert not work
    return out


def per_device_general(queries, keys, values, page_start):
    tok_rows, slab_width = queries.shape
    local_heads = slab_width // HD
    runs = lax.axis_size("dp")
    kv, per_kv = kv_of(keys, values, local_heads)
    run_index = lax.axis_index("dp")
    start = (page_start - run_index * tok_rows).reshape(tok_rows, 1)
    outputs = jnp.concatenate(
        [attend(queries, *kv[h // per_kv], start, h, per_kv) for h in range(0, local_heads, per_kv)], 1
    )
    steps = lax.axis_size("tensor") // 2 + 1
    rows = slab_width // runs
    moving = lax.all_gather(outputs, "dp", axis=0, tiled=True)
    left = lax.dynamic_slice_in_dim(moving, run_index * rows, rows, 1)
    tiles = []
    for offset in range(steps):
        if offset:
            moving = from_behind(moving, "tensor", -1)
        tiles.append(
            lax.dot_general(
                left, moving, (((0,), (0,)), ((), ())), preferred_element_type=jnp.float32
            )
        )
    return jnp.concatenate(tiles, 1) * (2.0 / (tok_rows * runs))


def solution(mesh):
    cores = mesh.shape["tensor"]
    rows = HEADS * HD // cores // mesh.shape["dp"]
    tuned = cores == 4 and rows % HD == 0
    return jax.shard_map(
        per_device if tuned else per_device_general,
        mesh=mesh,
        in_specs=(
            P(("groups", "dp"), "tensor"),
            P(("groups", "dp"), None),
            P(("groups", "dp"), None),
            P(("groups", "dp")),
        ),
        out_specs=P(("groups", "tensor", "dp"), None),
        check_vma=False,
    )
```

time: 1190 us -> 296 us (0.25)
  waiting for transfers between devices: 970 us -> 74.6 us
  Pallas kernels: 0 us -> 112 us
  matrix products: 84.5 us -> 0 us
  starting transfers between devices: 8.84 us -> 69.3 us
  other arithmetic: 79.4 us -> 33.1 us
  local copies, waits for them, and re-layouts: 34.9 us -> 5.11 us
  between operations: 13.5 us -> 0.57 us
    reduce_scatter x1 -> x0, waiting for transfers between devices: 923 us -> none  [per_device(): lax.psum_scatter(jnp.concatenate(tiles, 1).astype(jnp.bfloat16), 'dp', sc...]
    pallas_call x0 -> x18, Pallas kernels: none -> 112 us  [the longest x8 64.3 us: gram(): pl.pallas_call(functools.partial(gram_kernel, runs, places, starts, depth...]
    concatenate x3 -> x2, other arithmetic: 62.4 us -> 0.77 us  [kv_of(): own.append(jnp.concatenate(parts, 1))]
    dot_general x4 -> x0, matrix products: 58.4 us -> none  [the longest x3 41 us: per_device(): lax.dot_general(outputs, other, (((0,), (0,)), ((), ())), preferred_eleme...]
    ppermute x0 -> x42, starting transfers between devices: none -> 52.6 us  [over_tensor(): return lax.ppermute(value, 'tensor', [(t, t ^ bit) for t in range(count)])]
    ppermute x0 -> x42, waiting for transfers between devices: none -> 40.6 us  [over_tensor(): return lax.ppermute(value, 'tensor', [(t, t ^ bit) for t in range(count)])]
    select_n x0 -> x21, other arithmetic: none -> 32.3 us  [per_device(): sent = jnp.where(even, *[jnp.concatenate(x, 1) for x in pair])]
    mul x1 -> x0, local copies, waits for them, and re-layouts: 27.7 us -> none  [per_device(): return summed * (2.0 / total_tokens)]
  transfers between devices with their start and end apart: 5 -> 65, of which waited for: 4 -> 24; matrix products, arithmetic and copies ran while one was open for 3% -> 11% of each run, Pallas kernels for 0% -> 35%
where the time goes in v2:
time: 296 us; the launch traced here: 294 us
  Pallas kernels  112 us (38%)
  waiting for transfers between devices  74.6 us (25%)
  starting transfers between devices  69.3 us (23%)
  other arithmetic  33.1 us (11%)
  local copies, waits for them, and re-layouts  5.11 us (2%)
    pallas_call x8, Pallas kernels, gram(): pl.pallas_call(functools.partial(gram_kernel, runs, places, starts, depth...  64.3 us
    ppermute x42, starting transfers between devices, over_tensor(): return lax.ppermute(value, 'tensor', [(t, t ^ bit) for t in range(count)])  52.6 us
    ppermute x42, waiting for transfers between devices, over_tensor(): return lax.ppermute(value, 'tensor', [(t, t ^ bit) for t in range(count)])  40.6 us
    pallas_call x6, Pallas kernels, attend(): pl.pallas_call(attend_kernel, grid=(heads,), out_shape=jax.ShapeDtypeStru...  38.1 us
    ppermute x21, waiting for transfers between devices, from_behind(): return lax.ppermute(value, axis, pairs)  34 us
    select_n x21, other arithmetic, per_device(): sent = jnp.where(even, *[jnp.concatenate(x, 1) for x in pair])  32.3 us
    pallas_call x4, Pallas kernels, rows_of(): pl.pallas_call(functools.partial(rows_kernel, widths, rows), out_shape=ja...  9.41 us
    ppermute x21, starting transfers between devices, from_behind(): return lax.ppermute(value, axis, pairs)  8.77 us
  transfers between devices with their start and end apart: 65, of which 24 were waited for; matrix products, arithmetic and copies ran while one was open for 11% of the time, Pallas kernels for 35%

profile of v2, /device:TPU:1, one launch (start us, length us, event | category | flops | bytes accessed | tf_op | source)
XLA Modules:
  0.0 294.4 jit_solution(11847023545066209072)
XLA Ops:
  1.2 4.0 %collective-permute-start = (bf16[512,256]{1,0:T(8,128)(2,1)S(1)}, bf16[512,256]{1,0:T(8,128)(2,1)S(1)}, u32[]{:S(2)}, u32[]{:S(2)}) collective-permute-start(bf16[512,256]{1,0:T(8,128)(2,1)S(1)} %pad_maximum_fusion.ko_ref.vo_ref), channel_id=1, source_target_pairs={{0,1},{1,2},{2,3},{4,5},{5,6},{6,7},{8,9},{9,10},{10,11},{12,13},{... | collective-permute-start | bytes 786440 | tf_op jit(solution)/shard_map/ppermute | solution.py:22
  6.0 3.9 %collective-permute-start.2 = (bf16[512,256]{1,0:T(8,128)(2,1)}, bf16[512,256]{1,0:T(8,128)(2,1)}, u32[]{:S(2)}, u32[]{:S(2)}) collective-permute-start(bf16[512,256]{1,0:T(8,128)(2,1)} %pad_maximum_fusion.1.ko_ref.vo_ref), channel_id=1, source_target_pairs={{0,1},{1,2},{2,3},{4,5},{5,6},{6,7},{8,9},{9,10},{10,11},{12,13},{... | collective-permute-start | bytes 786440 | tf_op jit(solution)/shard_map/ppermute | solution.py:22
  11.5 6.3 %shard_map.46.refs_0_.refs_2_ = bf16[512,512]{1,0:T(8,128)(2,1)} custom-call(s32[512,1]{1,0:T(8,128)} %copy.12.start_ref, bf16[512,3072]{1,0:T(8,128)(2,1)} %q_ref.11, bf16[512,256]{1,0:T(8,128)(2,1)} %copy-done.17, bf16[512,256]{1,0:T(8,128)(2,1)} %copy-done.11, bf16[512,256]{1,0:T(8,128)(2,1)} %copy-done.17, bf16[512,256]{1,0:T(8,128)(2,1)} %copy-done.11), custom_call_target="tpu_custom_call" | custom-call | flops 999999986991104 | bytes 1 | tf_op jit(solution)/shard_map/pallas_call | solution.py:83
  22.2 6.4 %shard_map.49.refs_1_.refs_4_ = bf16[512,512]{1,0:T(8,128)(2,1)} custom-call(s32[512,1]{1,0:T(8,128)} %copy.15.start_ref, bf16[512,3072]{1,0:T(8,128)(2,1)} %q_ref.11, bf16[512,256]{1,0:T(8,128)(2,1)} %copy-done.17, bf16[512,256]{1,0:T(8,128)(2,1)} %copy-done.11, bf16[512,256]{1,0:T(8,128)(2,1)} %copy-done.17, bf16[512,256]{1,0:T(8,128)(2,1)} %copy-done.11), custom_call_target="tpu_custom_call" | custom-call | flops 999999986991104 | bytes 1 | tf_op jit(solution)/shard_map/pallas_call | solution.py:83
  32.1 5.9 %collective-permute-start.20 = (bf16[512,512]{1,0:T(8,128)(2,1)}, bf16[512,512]{1,0:T(8,128)(2,1)}, u32[]{:S(2)}, u32[]{:S(2)}) collective-permute-start(bf16[512,512]{1,0:T(8,128)(2,1)} %broadcast_select_fusion.17), channel_id=1, source_target_pairs={{0,4},{4,0},{8,12},{12,8},{1,5},{5,1},{9,13},{13,9},{2,6},{6,2},{1... | collective-permute-start | bytes 1572872 | tf_op jit(solution)/shard_map/ppermute | solution.py:33
  38.0 6.4 %shard_map.48.refs_2_.refs_6_ = bf16[512,512]{1,0:T(8,128)(2,1)} custom-call(s32[512,1]{1,0:T(8,128)} %copy.12.start_ref, bf16[512,3072]{1,0:T(8,128)(2,1)} %q_ref.11, bf16[512,256]{1,0:T(8,128)(2,1)} %copy-done.17, bf16[512,256]{1,0:T(8,128)(2,1)} %copy-done.11, bf16[512,256]{1,0:T(8,128)(2,1)} %copy-done.17, bf16[512,256]{1,0:T(8,128)(2,1)} %copy-done.11), custom_call_target="tpu_custom_call" | custom-call | flops 999999986991104 | bytes 1 | tf_op jit(solution)/shard_map/pallas_call | solution.py:83
  45.7 2.2 collective-permute-start.5
  50.4 6.4 %shard_map.51.refs_3_.refs_8_ = bf16[512,512]{1,0:T(8,128)(2,1)} custom-call(s32[512,1]{1,0:T(8,128)} %copy.12.start_ref, bf16[512,3072]{1,0:T(8,128)(2,1)} %q_ref.11, bf16[512,256]{1,0:T(8,128)(2,1)} %collective-permute-done.2.kp_ref.vp_ref, bf16[512,256]{1,0:T(8,128)(2,1)} %pad_maximum_fusion.1.ko_ref.vo_ref, ...), custom_call_target="tpu_custom_call" | custom-call | flops 999999986991104 | bytes 1 | tf_op jit(solution)/shard_map/pallas_call | solution.py:83
  58.1 2.0 collective-permute-done.4.refs_2_.refs_7_
  61.1 1.8 collective-permute-start.22
  63.0 6.3 %shard_map.47.refs_4_.refs_10_ = bf16[512,512]{1,0:T(8,128)(2,1)} custom-call(s32[512,1]{1,0:T(8,128)} %copy.12.start_ref, bf16[512,3072]{1,0:T(8,128)(2,1)} %q_ref.11, bf16[512,256]{1,0:T(8,128)(2,1)} %collective-permute-done.2.kp_ref.vp_ref, bf16[512,256]{1,0:T(8,128)(2,1)} %pad_maximum_fusion.1.ko_ref.vo_ref, ...), custom_call_target="tpu_custom_call" | custom-call | flops 999999986991104 | bytes 1 | tf_op jit(solution)/shard_map/pallas_call | solution.py:83
  71.0 1.7 collective-permute-start.7
  75.2 6.3 %shard_map.50.refs_5_.refs_12_ = bf16[512,512]{1,0:T(8,128)(2,1)} custom-call(s32[512,1]{1,0:T(8,128)} %copy.12.start_ref, bf16[512,3072]{1,0:T(8,128)(2,1)} %q_ref.11, bf16[512,256]{1,0:T(8,128)(2,1)} %collective-permute-done.2.kp_ref.vp_ref, bf16[512,256]{1,0:T(8,128)(2,1)} %pad_maximum_fusion.1.ko_ref.vo_ref, ...), custom_call_target="tpu_custom_call" | custom-call | flops 999999986991104 | bytes 1 | tf_op jit(solution)/shard_map/pallas_call | solution.py:83
  86.0 2.2 collective-permute-start.24
  88.3 2.4 shard_map.52.refs_0_
  90.7 2.1 collective-permute-start.16
  92.8 4.5 %collective-permute-done.13.refs_5_.refs_13_ = bf16[512,512]{1,0:T(8,128)(2,1)} collective-permute-done((bf16[512,512]{1,0:T(8,128)(2,1)}, bf16[512,512]{1,0:T(8,128)(2,1)}, u32[]{:S(2)}, u32[]{:S(2)}) %collective-permute-start.13) | collective-permute-done | bytes 524320 | tf_op jit(solution)/shard_map/ppermute | solution.py:28
  99.5 2.3 collective-permute-start.25
  101.8 2.3 shard_map.53.refs_1_
  104.2 3.5 %collective-permute-done.16.refs_3_ = bf16[512,512]{1,0:T(8,128)(2,1)} collective-permute-done((bf16[512,512]{1,0:T(8,128)(2,1)}, bf16[512,512]{1,0:T(8,128)(2,1)}, u32[]{:S(2)}, u32[]{:S(2)}) %collective-permute-start.16) | collective-permute-done | bytes 524320 | tf_op jit(solution)/shard_map/ppermute | solution.py:33
  108.2 1.9 broadcast_select_fusion.11
  111.9 8.9 %shard_map.54.refs_10_ = f32[768,9216]{1,0:T(8,128)} custom-call(bf16[768,512]{1,0:T(8,128)(2,1)} %shard_map.52.refs_0_, bf16[768,512]{1,0:T(8,128)(2,1)} %shard_map.53.refs_1_, bf16[512,512]{1,0:T(8,128)(2,1)} %shard_map.46.refs_0_.refs_2_, bf16[512,512]{1,0:T(8,128)(2,1)} %collective-permute-done.1.refs_0_.refs_3_, ...), custom_call_target="tpu_custom_call" | custom-call | flops 999999986991104 | bytes 1 | tf_op jit(solution)/shard_map/pallas_call | solution.py:238
  125.1 11.5 %collective-permute-done.17.refs_2_.refs_6_ = bf16[512,512]{1,0:T(8,128)(2,1)} collective-permute-done((bf16[512,512]{1,0:T(8,128)(2,1)}, bf16[512,512]{1,0:T(8,128)(2,1)}, u32[]{:S(2)}, u32[]{:S(2)}) %collective-permute-start.17) | collective-permute-done | bytes 524320 | tf_op jit(solution)/shard_map/ppermute | solution.py:28
  137.5 2.1 broadcast_select_fusion.9
  139.9 7.0 %shard_map.55.refs_10_ = f32[768,9216]{1,0:T(8,128)} custom-call(bf16[768,512]{1,0:T(8,128)(2,1)} %shard_map.52.refs_0_, bf16[768,512]{1,0:T(8,128)(2,1)} %shard_map.53.refs_1_, bf16[512,512]{1,0:T(8,128)(2,1)} %collective-permute-done.3.refs_2_, bf16[512,512]{1,0:T(8,128)(2,1)} %collective-permute-done.16.refs_3_, ...), custom_call_target="tpu_custom_call", output_to_operand_aliasing={{}: (10, {})} | custom-call | flops 999999986991104 | bytes 1 | tf_op jit(solution)/shard_map/pallas_call | solution.py:238
  151.1 6.2 %collective-permute-done.33.refs_3_ = bf16[512,512]{1,0:T(8,128)(2,1)} collective-permute-done((bf16[512,512]{1,0:T(8,128)(2,1)}, bf16[512,512]{1,0:T(8,128)(2,1)}, u32[]{:S(2)}, u32[]{:S(2)}) %collective-permute-start.33) | collective-permute-done | bytes 524320 | tf_op jit(solution)/shard_map/ppermute | solution.py:33
  159.9 2.1 broadcast_select_fusion.7
  163.5 7.0 %shard_map.57.refs_10_ = f32[768,9216]{1,0:T(8,128)} custom-call(bf16[768,512]{1,0:T(8,128)(2,1)} %shard_map.52.refs_0_, bf16[768,512]{1,0:T(8,128)(2,1)} %shard_map.53.refs_1_, bf16[512,512]{1,0:T(8,128)(2,1)} %collective-permute-done.5.refs_2_, bf16[512,512]{1,0:T(8,128)(2,1)} %copy-done.4, ...), custom_call_target="tpu_custom_call", output_to_operand_aliasing={{}: (10, {})} | custom-call | flops 999999986991104 | bytes 1 | tf_op jit(solution)/shard_map/pallas_call | solution.py:238
  173.5 6.2 %collective-permute-done.39.refs_2_ = bf16[512,512]{1,0:T(8,128)(2,1)} collective-permute-done((bf16[512,512]{1,0:T(8,128)(2,1)}, bf16[512,512]{1,0:T(8,128)(2,1)}, u32[]{:S(2)}, u32[]{:S(2)}) %collective-permute-start.39) | collective-permute-done | bytes 524320 | tf_op jit(solution)/shard_map/ppermute | solution.py:33
  182.4 2.1 broadcast_select_fusion.5
  186.0 7.0 %shard_map.58.refs_14_ = f32[768,9216]{1,0:T(8,128)} custom-call(bf16[768,512]{1,0:T(8,128)(2,1)} %shard_map.52.refs_0_, bf16[768,512]{1,0:T(8,128)(2,1)} %shard_map.53.refs_1_, bf16[512,512]{1,0:T(8,128)(2,1)} %collective-permute-done.7.refs_2_, bf16[512,512]{1,0:T(8,128)(2,1)} %collective-permute-done.33.refs_3_, ...), custom_call_target="tpu_custom_call", output_to_operand_aliasing={{}: (10, {})} | custom-call | flops 999999986991104 | bytes 1 | tf_op jit(solution)/shard_map/pallas_call | solution.py:238
  196.0 6.2 %collective-permute-done.45.refs_2_ = bf16[512,512]{1,0:T(8,128)(2,1)} collective-permute-done((bf16[512,512]{1,0:T(8,128)(2,1)}, bf16[512,512]{1,0:T(8,128)(2,1)}, u32[]{:S(2)}, u32[]{:S(2)}) %collective-permute-start.45) | collective-permute-done | bytes 524320 | tf_op jit(solution)/shard_map/ppermute | solution.py:33
  207.2 6.2 %collective-permute-done.48.refs_6_ = bf16[512,512]{1,0:T(8,128)(2,1)} collective-permute-done((bf16[512,512]{1,0:T(8,128)(2,1)}, bf16[512,512]{1,0:T(8,128)(2,1)}, u32[]{:S(2)}, u32[]{:S(2)}) %collective-permute-start.48) | collective-permute-done | bytes 524320 | tf_op jit(solution)/shard_map/ppermute | solution.py:33
  215.9 1.9 broadcast_select_fusion.2
  218.9 2.3 shard_map.56.refs_0_
  222.3 2.4 collective-permute-done.51.refs_6_
  229.4 6.6 %collective-permute-done.50.refs_6_ = bf16[512,512]{1,0:T(8,128)(2,1)} collective-permute-done((bf16[512,512]{1,0:T(8,128)(2,1)}, bf16[512,512]{1,0:T(8,128)(2,1)}, u32[]{:S(2)}, u32[]{:S(2)}) %collective-permute-start.50) | collective-permute-done | bytes 524320 | tf_op jit(solution)/shard_map/ppermute | solution.py:33
  237.5 2.1 broadcast_select_fusion
  239.6 1.8 collective-permute-start.59
  241.4 2.4 shard_map.59.refs_1_
  244.4 2.7 collective-permute-done.56.refs_3_
  249.6 2.6 maximum_select_fusion
  253.6 11.0 %shard_map.60.refs_10_ = f32[768,9216]{1,0:T(8,128)} custom-call(bf16[768,512]{1,0:T(8,128)(2,1)} %shard_map.56.refs_0_, bf16[768,512]{1,0:T(8,128)(2,1)} %shard_map.59.refs_1_, bf16[512,512]{1,0:T(8,128)(2,1)} %collective-permute-done.8.refs_0_.refs_2_, bf16[512,512]{1,0:T(8,128)(2,1)} %collective-permute-done.34.refs_0_.refs_3_, ...), custom_call_target="tpu_custom_call", output_to_operand_aliasing={{}: (14, {})} | custom-call | flops 999999986991104 | bytes 1 | tf_op jit(solution)/shard_map/pallas_call | solution.py:238
  264.6 2.9 maximum_select_fusion.1
  267.5 7.9 %shard_map.61.refs_10_ = f32[768,9216]{1,0:T(8,128)} custom-call(bf16[768,512]{1,0:T(8,128)(2,1)} %shard_map.56.refs_0_, bf16[768,512]{1,0:T(8,128)(2,1)} %shard_map.59.refs_1_, bf16[512,512]{1,0:T(8,128)(2,1)} %collective-permute-done.39.refs_2_, bf16[512,512]{1,0:T(8,128)(2,1)} %collective-permute-done.56.refs_3_, ...), custom_call_target="tpu_custom_call", output_to_operand_aliasing={{}: (10, {})} | custom-call | flops 999999986991104 | bytes 1 | tf_op jit(solution)/shard_map/pallas_call | solution.py:238
  275.4 2.7 maximum_select_fusion.2
  278.6 7.8 %shard_map.62.refs_10_ = f32[768,9216]{1,0:T(8,128)} custom-call(bf16[768,512]{1,0:T(8,128)(2,1)} %shard_map.56.refs_0_, bf16[768,512]{1,0:T(8,128)(2,1)} %shard_map.59.refs_1_, bf16[512,512]{1,0:T(8,128)(2,1)} %collective-permute-done.42.refs_2_, bf16[512,512]{1,0:T(8,128)(2,1)} %collective-permute-done.61.refs_3_, ...), custom_call_target="tpu_custom_call", output_to_operand_aliasing={{}: (10, {})} | custom-call | flops 999999986991104 | bytes 1 | tf_op jit(solution)/shard_map/pallas_call | solution.py:238
  286.4 7.8 %shard_map.63 = f32[768,9216]{1,0:T(8,128)} custom-call(bf16[768,512]{1,0:T(8,128)(2,1)} %shard_map.56.refs_0_, bf16[768,512]{1,0:T(8,128)(2,1)} %shard_map.59.refs_1_, bf16[512,512]{1,0:T(8,128)(2,1)} %collective-permute-done.45.refs_2_, bf16[512,512]{1,0:T(8,128)(2,1)} %collective-permute-done.57.refs_3_, ...), custom_call_target="tpu_custom_call", output_to_operand_aliasing={{}: (10, {})} | custom-call | flops 999999986991104 | bytes 1 | tf_op jit(solution)/shard_map/pallas_call | solution.py:238
  (163 shorter events, 75.5 us)
Async XLA Ops:
  6.0 14.6 %collective-permute-start.2 = (bf16[512,256]{1,0:T(8,128)(2,1)}, bf16[512,256]{1,0:T(8,128)(2,1)}, u32[]{:S(2)}, u32[]{:S(2)}) collective-permute-start(bf16[512,256]{1,0:T(8,128)(2,1)} %pad_maximum_fusion.1.ko_ref.vo_ref), channel_id=1, source_target_pairs={{0,1},{1,2},{2,3},{4,5},{5,6},{6,7},{8,9},{9,10},{10,11},{12,13},{... | collective-permute-start | bytes 786440 | tf_op jit(solution)/shard_map/ppermute | solution.py:22
  17.7 13.5 %collective-permute-start.1 = (bf16[512,512]{1,0:T(8,128)(2,1)}, bf16[512,512]{1,0:T(8,128)(2,1)}, u32[]{:S(2)}, u32[]{:S(2)}) collective-permute-start(bf16[512,512]{1,0:T(8,128)(2,1)} %shard_map.46.refs_0_.refs_2_), channel_id=1, source_target_pairs={{0,1},{1,2},{2,3},{3,0},{4,5},{5,6},{6,7},{7,4},{8,9},{9,10},{10,1... | collective-permute-start | bytes 1572872 | tf_op jit(solution)/shard_map/ppermute | solution.py:28
  19.4 11.9 %collective-permute-start.3 = (bf16[512,512]{1,0:T(8,128)(2,1)}, bf16[512,512]{1,0:T(8,128)(2,1)}, u32[]{:S(2)}, u32[]{:S(2)}) collective-permute-start(bf16[512,512]{1,0:T(8,128)(2,1)} %shard_map.46.refs_0_.refs_2_), channel_id=1, source_target_pairs={{0,8},{4,12},{8,0},{12,4},{1,9},{5,13},{9,1},{13,5},{2,10},{6,14},... | collective-permute-start | bytes 1572872 | tf_op jit(solution)/shard_map/ppermute | solution.py:33
  28.5 19.3 %collective-permute-start.10 = (bf16[512,512]{1,0:T(8,128)(2,1)}, bf16[512,512]{1,0:T(8,128)(2,1)}, u32[]{:S(2)}, u32[]{:S(2)}) collective-permute-start(bf16[512,512]{1,0:T(8,128)(2,1)} %shard_map.49.refs_1_.refs_4_), channel_id=1, source_target_pairs={{0,8},{4,12},{8,0},{12,4},{1,9},{5,13},{9,1},{13,5},{2,10},{6,14},... | collective-permute-start | bytes 1572872 | tf_op jit(solution)/shard_map/ppermute | solution.py:33
  28.8 19.1 %collective-permute-start.9 = (bf16[512,512]{1,0:T(8,128)(2,1)}, bf16[512,512]{1,0:T(8,128)(2,1)}, u32[]{:S(2)}, u32[]{:S(2)}) collective-permute-start(bf16[512,512]{1,0:T(8,128)(2,1)} %shard_map.49.refs_1_.refs_4_), channel_id=1, source_target_pairs={{0,1},{1,2},{2,3},{3,0},{4,5},{5,6},{6,7},{7,4},{8,9},{9,10},{10,1... | collective-permute-start | bytes 1572872 | tf_op jit(solution)/shard_map/ppermute | solution.py:28
  32.1 15.7 %collective-permute-start.20 = (bf16[512,512]{1,0:T(8,128)(2,1)}, bf16[512,512]{1,0:T(8,128)(2,1)}, u32[]{:S(2)}, u32[]{:S(2)}) collective-permute-start(bf16[512,512]{1,0:T(8,128)(2,1)} %broadcast_select_fusion.17), channel_id=1, source_target_pairs={{0,4},{4,0},{8,12},{12,8},{1,5},{5,1},{9,13},{13,9},{2,6},{6,2},{1... | collective-permute-start | bytes 1572872 | tf_op jit(solution)/shard_map/ppermute | solution.py:33
  44.4 15.7 %collective-permute-start.4 = (bf16[512,512]{1,0:T(8,128)(2,1)}, bf16[512,512]{1,0:T(8,128)(2,1)}, u32[]{:S(2)}, u32[]{:S(2)}) collective-permute-start(bf16[512,512]{1,0:T(8,128)(2,1)} %shard_map.48.refs_2_.refs_6_), channel_id=1, source_target_pairs={{0,1},{1,2},{2,3},{3,0},{4,5},{5,6},{6,7},{7,4},{8,9},{9,10},{10,1... | collective-permute-start | bytes 1572872 | tf_op jit(solution)/shard_map/ppermute | solution.py:28
  45.7 14.6 %collective-permute-start.5 = (bf16[512,512]{1,0:T(8,128)(2,1)}, bf16[512,512]{1,0:T(8,128)(2,1)}, u32[]{:S(2)}, u32[]{:S(2)}) collective-permute-start(bf16[512,512]{1,0:T(8,128)(2,1)} %shard_map.48.refs_2_.refs_6_), channel_id=1, source_target_pairs={{0,8},{4,12},{8,0},{12,4},{1,9},{5,13},{9,1},{13,5},{2,10},{6,14},... | collective-permute-start | bytes 1572872 | tf_op jit(solution)/shard_map/ppermute | solution.py:33
  56.7 16.0 %collective-permute-start.11 = (bf16[512,512]{1,0:T(8,128)(2,1)}, bf16[512,512]{1,0:T(8,128)(2,1)}, u32[]{:S(2)}, u32[]{:S(2)}) collective-permute-start(bf16[512,512]{1,0:T(8,128)(2,1)} %shard_map.51.refs_3_.refs_8_), channel_id=1, source_target_pairs={{0,1},{1,2},{2,3},{3,0},{4,5},{5,6},{6,7},{7,4},{8,9},{9,10},{10,1... | collective-permute-start | bytes 1572872 | tf_op jit(solution)/shard_map/ppermute | solution.py:28
  58.0 14.7 %collective-permute-start.12 = (bf16[512,512]{1,0:T(8,128)(2,1)}, bf16[512,512]{1,0:T(8,128)(2,1)}, u32[]{:S(2)}, u32[]{:S(2)}) collective-permute-start(bf16[512,512]{1,0:T(8,128)(2,1)} %shard_map.51.refs_3_.refs_8_), channel_id=1, source_target_pairs={{0,8},{4,12},{8,0},{12,4},{1,9},{5,13},{9,1},{13,5},{2,10},{6,14},... | collective-permute-start | bytes 1572872 | tf_op jit(solution)/shard_map/ppermute | solution.py:33
  69.3 15.7 %collective-permute-start.6 = (bf16[512,512]{1,0:T(8,128)(2,1)}, bf16[512,512]{1,0:T(8,128)(2,1)}, u32[]{:S(2)}, u32[]{:S(2)}) collective-permute-start(bf16[512,512]{1,0:T(8,128)(2,1)} %shard_map.47.refs_4_.refs_10_), channel_id=1, source_target_pairs={{0,1},{1,2},{2,3},{3,0},{4,5},{5,6},{6,7},{7,4},{8,9},{9,10},{10,1... | collective-permute-start | bytes 1572872 | tf_op jit(solution)/shard_map/ppermute | solution.py:28
  71.0 14.2 %collective-permute-start.7 = (bf16[512,512]{1,0:T(8,128)(2,1)}, bf16[512,512]{1,0:T(8,128)(2,1)}, u32[]{:S(2)}, u32[]{:S(2)}) collective-permute-start(bf16[512,512]{1,0:T(8,128)(2,1)} %shard_map.47.refs_4_.refs_10_), channel_id=1, source_target_pairs={{0,8},{4,12},{8,0},{12,4},{1,9},{5,13},{9,1},{13,5},{2,10},{6,14},... | collective-permute-start | bytes 1572872 | tf_op jit(solution)/shard_map/ppermute | solution.py:33
  81.6 15.7 %collective-permute-start.13 = (bf16[512,512]{1,0:T(8,128)(2,1)}, bf16[512,512]{1,0:T(8,128)(2,1)}, u32[]{:S(2)}, u32[]{:S(2)}) collective-permute-start(bf16[512,512]{1,0:T(8,128)(2,1)} %shard_map.50.refs_5_.refs_12_), channel_id=1, source_target_pairs={{0,1},{1,2},{2,3},{3,0},{4,5},{5,6},{6,7},{7,4},{8,9},{9,10},{10,1... | collective-permute-start | bytes 1572872 | tf_op jit(solution)/shard_map/ppermute | solution.py:28
  81.8 15.4 %collective-permute-start.14 = (bf16[512,512]{1,0:T(8,128)(2,1)}, bf16[512,512]{1,0:T(8,128)(2,1)}, u32[]{:S(2)}, u32[]{:S(2)}) collective-permute-start(bf16[512,512]{1,0:T(8,128)(2,1)} %shard_map.50.refs_5_.refs_12_), channel_id=1, source_target_pairs={{0,8},{4,12},{8,0},{12,4},{1,9},{5,13},{9,1},{13,5},{2,10},{6,14},... | collective-permute-start | bytes 1572872 | tf_op jit(solution)/shard_map/ppermute | solution.py:33
  86.0 12.6 %collective-permute-start.24 = (bf16[512,512]{1,0:T(8,128)(2,1)}, bf16[512,512]{1,0:T(8,128)(2,1)}, u32[]{:S(2)}, u32[]{:S(2)}) collective-permute-start(bf16[512,512]{1,0:T(8,128)(2,1)} %broadcast_select_fusion.13), channel_id=1, source_target_pairs={{0,4},{4,0},{8,12},{12,8},{1,5},{5,1},{9,13},{13,9},{2,6},{6,2},{1... | collective-permute-start | bytes 1572872 | tf_op jit(solution)/shard_map/ppermute | solution.py:33
  90.7 17.0 %collective-permute-start.16 = (bf16[512,512]{1,0:T(8,128)(2,1)}, bf16[512,512]{1,0:T(8,128)(2,1)}, u32[]{:S(2)}, u32[]{:S(2)}) collective-permute-start(bf16[512,512]{1,0:T(8,128)(2,1)} %collective-permute-done.1.refs_0_.refs_3_), channel_id=1, source_target_pairs={{0,8},{4,12},{8,0},{12,4},{1,9},{5,13},{9,1},{13,5},{2,10},{6,14},... | collective-permute-start | bytes 1572872 | tf_op jit(solution)/shard_map/ppermute | solution.py:33
  92.8 15.4 %collective-permute-start.8 = (bf16[512,512]{1,0:T(8,128)(2,1)}, bf16[512,512]{1,0:T(8,128)(2,1)}, u32[]{:S(2)}, u32[]{:S(2)}) collective-permute-start(bf16[512,512]{1,0:T(8,128)(2,1)} %collective-permute-done.1.refs_0_.refs_3_), channel_id=1, source_target_pairs={{0,1},{1,2},{2,3},{3,0},{4,5},{5,6},{6,7},{7,4},{8,9},{9,10},{10,1... | collective-permute-start | bytes 1572872 | tf_op jit(solution)/shard_map/ppermute | solution.py:28
  97.2 24.6 %collective-permute-start.15 = (bf16[512,512]{1,0:T(8,128)(2,1)}, bf16[512,512]{1,0:T(8,128)(2,1)}, u32[]{:S(2)}, u32[]{:S(2)}) collective-permute-start(bf16[512,512]{1,0:T(8,128)(2,1)} %collective-permute-done.9.refs_1_.refs_5_), channel_id=1, source_target_pairs={{0,1},{1,2},{2,3},{3,0},{4,5},{5,6},{6,7},{7,4},{8,9},{9,10},{10,1... | collective-permute-start | bytes 1572872 | tf_op jit(solution)/shard_map/ppermute | solution.py:28
  97.3 24.6 %collective-permute-start.18 = (bf16[512,512]{1,0:T(8,128)(2,1)}, bf16[512,512]{1,0:T(8,128)(2,1)}, u32[]{:S(2)}, u32[]{:S(2)}) collective-permute-start(bf16[512,512]{1,0:T(8,128)(2,1)} %collective-permute-done.9.refs_1_.refs_5_), channel_id=1, source_target_pairs={{0,8},{4,12},{8,0},{12,4},{1,9},{5,13},{9,1},{13,5},{2,10},{6,14},... | collective-permute-start | bytes 1572872 | tf_op jit(solution)/shard_map/ppermute | solution.py:33
  110.1 11.7 %collective-permute-start.26 = (bf16[512,512]{1,0:T(8,128)(2,1)}, bf16[512,512]{1,0:T(8,128)(2,1)}, u32[]{:S(2)}, u32[]{:S(2)}) collective-permute-start(bf16[512,512]{1,0:T(8,128)(2,1)} %broadcast_select_fusion.11), channel_id=1, source_target_pairs={{0,4},{4,0},{8,12},{12,8},{1,5},{5,1},{9,13},{13,9},{2,6},{6,2},{1... | collective-permute-start | bytes 1572872 | tf_op jit(solution)/shard_map/ppermute | solution.py:33
  120.8 15.7 %collective-permute-start.17 = (bf16[512,512]{1,0:T(8,128)(2,1)}, bf16[512,512]{1,0:T(8,128)(2,1)}, u32[]{:S(2)}, u32[]{:S(2)}) collective-permute-start(bf16[512,512]{1,0:T(8,128)(2,1)} %collective-permute-done.4.refs_2_.refs_7_), channel_id=1, source_target_pairs={{0,1},{1,2},{2,3},{3,0},{4,5},{5,6},{6,7},{7,4},{8,9},{9,10},{10,1... | collective-permute-start | bytes 1572872 | tf_op jit(solution)/shard_map/ppermute | solution.py:28
  120.9 15.7 %collective-permute-start.27 = (bf16[512,512]{1,0:T(8,128)(2,1)}, bf16[512,512]{1,0:T(8,128)(2,1)S(1)}, u32[]{:S(2)}, u32[]{:S(2)}) collective-permute-start(bf16[512,512]{1,0:T(8,128)(2,1)} %collective-permute-done.4.refs_2_.refs_7_), channel_id=1, source_target_pairs={{0,8},{4,12},{8,0},{12,4},{1,9},{5,13},{9,1},{13,5},{2,10},{6,14},... | collective-permute-start | bytes 1572872 | tf_op jit(solution)/shard_map/ppermute | solution.py:33
  123.0 14.5 %collective-permute-start.29 = (bf16[512,512]{1,0:T(8,128)(2,1)S(1)}, bf16[512,512]{1,0:T(8,128)(2,1)S(1)}, u32[]{:S(2)}, u32[]{:S(2)}) collective-permute-start(bf16[512,512]{1,0:T(8,128)(2,1)S(1)} %broadcast_select_fusion.10), channel_id=1, source_target_pairs={{0,4},{4,0},{8,12},{12,8},{1,5},{5,1},{9,13},{13,9},{2,6},{6,2},{1... | collective-permute-start | bytes 1572872 | tf_op jit(solution)/shard_map/ppermute | solution.py:33
  123.3 23.5 %collective-permute-start.30 = (bf16[512,512]{1,0:T(8,128)(2,1)}, bf16[512,512]{1,0:T(8,128)(2,1)}, u32[]{:S(2)}, u32[]{:S(2)}) collective-permute-start(bf16[512,512]{1,0:T(8,128)(2,1)} %collective-permute-done.11.refs_3_.refs_9_), channel_id=1, source_target_pairs={{0,8},{4,12},{8,0},{12,4},{1,9},{5,13},{9,1},{13,5},{2,10},{6,14},... | collective-permute-start | bytes 1572872 | tf_op jit(solution)/shard_map/ppermute | solution.py:33
  123.9 23.9 %collective-permute-start.19 = (bf16[512,512]{1,0:T(8,128)(2,1)}, bf16[512,512]{1,0:T(8,128)(2,1)}, u32[]{:S(2)}, u32[]{:S(2)}) collective-permute-start(bf16[512,512]{1,0:T(8,128)(2,1)} %collective-permute-done.11.refs_3_.refs_9_), channel_id=1, source_target_pairs={{0,1},{1,2},{2,3},{3,0},{4,5},{5,6},{6,7},{7,4},{8,9},{9,10},{10,1... | collective-permute-start | bytes 1572872 | tf_op jit(solution)/shard_map/ppermute | solution.py:28
  136.5 20.7 %collective-permute-start.33 = (bf16[512,512]{1,0:T(8,128)(2,1)}, bf16[512,512]{1,0:T(8,128)(2,1)}, u32[]{:S(2)}, u32[]{:S(2)}) collective-permute-start(bf16[512,512]{1,0:T(8,128)(2,1)} %collective-permute-done.6.refs_4_.refs_11_), channel_id=1, source_target_pairs={{0,8},{4,12},{8,0},{12,4},{1,9},{5,13},{9,1},{13,5},{2,10},{6,14},... | collective-permute-start | bytes 1572872 | tf_op jit(solution)/shard_map/ppermute | solution.py:33
  137.5 21.5 %collective-permute-start.28 = (bf16[512,512]{1,0:T(8,128)(2,1)}, bf16[512,512]{1,0:T(8,128)(2,1)}, u32[]{:S(2)}, u32[]{:S(2)}) collective-permute-start(bf16[512,512]{1,0:T(8,128)(2,1)} %collective-permute-done.6.refs_4_.refs_11_), channel_id=1, source_target_pairs={{0,1},{1,2},{2,3},{3,0},{4,5},{5,6},{6,7},{7,4},{8,9},{9,10},{10,1... | collective-permute-start | bytes 1572872 | tf_op jit(solution)/shard_map/ppermute | solution.py:28
  150.1 20.4 %collective-permute-start.36 = (bf16[512,512]{1,0:T(8,128)(2,1)}, bf16[512,512]{1,0:T(8,128)(2,1)}, u32[]{:S(2)}, u32[]{:S(2)}) collective-permute-start(bf16[512,512]{1,0:T(8,128)(2,1)} %collective-permute-done.13.refs_5_.refs_13_), channel_id=1, source_target_pairs={{0,8},{4,12},{8,0},{12,4},{1,9},{5,13},{9,1},{13,5},{2,10},{6,14},... | collective-permute-start | bytes 1572872 | tf_op jit(solution)/shard_map/ppermute | solution.py:33
  151.1 19.5 %collective-permute-start.31 = (bf16[512,512]{1,0:T(8,128)(2,1)}, bf16[512,512]{1,0:T(8,128)(2,1)}, u32[]{:S(2)}, u32[]{:S(2)}) collective-permute-start(bf16[512,512]{1,0:T(8,128)(2,1)} %collective-permute-done.13.refs_5_.refs_13_), channel_id=1, source_target_pairs={{0,1},{1,2},{2,3},{3,0},{4,5},{5,6},{6,7},{7,4},{8,9},{9,10},{10,1... | collective-permute-start | bytes 1572872 | tf_op jit(solution)/shard_map/ppermute | solution.py:28
  159.0 20.8 %collective-permute-start.39 = (bf16[512,512]{1,0:T(8,128)(2,1)}, bf16[512,512]{1,0:T(8,128)(2,1)}, u32[]{:S(2)}, u32[]{:S(2)}) collective-permute-start(bf16[512,512]{1,0:T(8,128)(2,1)} %collective-permute-done.8.refs_0_.refs_2_), channel_id=1, source_target_pairs={{0,8},{4,12},{8,0},{12,4},{1,9},{5,13},{9,1},{13,5},{2,10},{6,14},... | collective-permute-start | bytes 1572872 | tf_op jit(solution)/shard_map/ppermute | solution.py:33
  159.9 21.5 %collective-permute-start.34 = (bf16[512,512]{1,0:T(8,128)(2,1)}, bf16[512,512]{1,0:T(8,128)(2,1)}, u32[]{:S(2)}, u32[]{:S(2)}) collective-permute-start(bf16[512,512]{1,0:T(8,128)(2,1)} %collective-permute-done.8.refs_0_.refs_2_), channel_id=1, source_target_pairs={{0,1},{1,2},{2,3},{3,0},{4,5},{5,6},{6,7},{7,4},{8,9},{9,10},{10,1... | collective-permute-start | bytes 1572872 | tf_op jit(solution)/shard_map/ppermute | solution.py:28
  172.6 20.4 %collective-permute-start.42 = (bf16[512,512]{1,0:T(8,128)(2,1)}, bf16[512,512]{1,0:T(8,128)(2,1)}, u32[]{:S(2)}, u32[]{:S(2)}) collective-permute-start(bf16[512,512]{1,0:T(8,128)(2,1)} %collective-permute-done.15.refs_1_.refs_4_), channel_id=1, source_target_pairs={{0,8},{4,12},{8,0},{12,4},{1,9},{5,13},{9,1},{13,5},{2,10},{6,14},... | collective-permute-start | bytes 1572872 | tf_op jit(solution)/shard_map/ppermute | solution.py:33
  173.5 19.5 %collective-permute-start.37 = (bf16[512,512]{1,0:T(8,128)(2,1)}, bf16[512,512]{1,0:T(8,128)(2,1)}, u32[]{:S(2)}, u32[]{:S(2)}) collective-permute-start(bf16[512,512]{1,0:T(8,128)(2,1)} %collective-permute-done.15.refs_1_.refs_4_), channel_id=1, source_target_pairs={{0,1},{1,2},{2,3},{3,0},{4,5},{5,6},{6,7},{7,4},{8,9},{9,10},{10,1... | collective-permute-start | bytes 1572872 | tf_op jit(solution)/shard_map/ppermute | solution.py:28
  181.5 20.8 %collective-permute-start.45 = (bf16[512,512]{1,0:T(8,128)(2,1)}, bf16[512,512]{1,0:T(8,128)(2,1)}, u32[]{:S(2)}, u32[]{:S(2)}) collective-permute-start(bf16[512,512]{1,0:T(8,128)(2,1)} %collective-permute-done.17.refs_2_.refs_6_), channel_id=1, source_target_pairs={{0,8},{4,12},{8,0},{12,4},{1,9},{5,13},{9,1},{13,5},{2,10},{6,14},... | collective-permute-start | bytes 1572872 | tf_op jit(solution)/shard_map/ppermute | solution.py:33
  182.4 21.5 %collective-permute-start.40 = (bf16[512,512]{1,0:T(8,128)(2,1)}, bf16[512,512]{1,0:T(8,128)(2,1)}, u32[]{:S(2)}, u32[]{:S(2)}) collective-permute-start(bf16[512,512]{1,0:T(8,128)(2,1)} %collective-permute-done.17.refs_2_.refs_6_), channel_id=1, source_target_pairs={{0,1},{1,2},{2,3},{3,0},{4,5},{5,6},{6,7},{7,4},{8,9},{9,10},{10,1... | collective-permute-start | bytes 1572872 | tf_op jit(solution)/shard_map/ppermute | solution.py:28
  195.0 18.4 %collective-permute-start.48 = (bf16[512,512]{1,0:T(8,128)(2,1)}, bf16[512,512]{1,0:T(8,128)(2,1)}, u32[]{:S(2)}, u32[]{:S(2)}) collective-permute-start(bf16[512,512]{1,0:T(8,128)(2,1)} %collective-permute-done.19.refs_3_.refs_8_), channel_id=1, source_target_pairs={{0,8},{4,12},{8,0},{12,4},{1,9},{5,13},{9,1},{13,5},{2,10},{6,14},... | collective-permute-start | bytes 1572872 | tf_op jit(solution)/shard_map/ppermute | solution.py:33
  196.0 19.1 %collective-permute-start.43 = (bf16[512,512]{1,0:T(8,128)(2,1)}, bf16[512,512]{1,0:T(8,128)(2,1)S(1)}, u32[]{:S(2)}, u32[]{:S(2)}) collective-permute-start(bf16[512,512]{1,0:T(8,128)(2,1)} %collective-permute-done.19.refs_3_.refs_8_), channel_id=1, source_target_pairs={{0,1},{1,2},{2,3},{3,0},{4,5},{5,6},{6,7},{7,4},{8,9},{9,10},{10,1... | collective-permute-start | bytes 1572872 | tf_op jit(solution)/shard_map/ppermute | solution.py:28
  206.3 18.4 %collective-permute-start.51 = (bf16[512,512]{1,0:T(8,128)(2,1)}, bf16[512,512]{1,0:T(8,128)(2,1)}, u32[]{:S(2)}, u32[]{:S(2)}) collective-permute-start(bf16[512,512]{1,0:T(8,128)(2,1)} %collective-permute-done.28.refs_4_.refs_10_), channel_id=1, source_target_pairs={{0,8},{4,12},{8,0},{12,4},{1,9},{5,13},{9,1},{13,5},{2,10},{6,14},... | collective-permute-start | bytes 1572872 | tf_op jit(solution)/shard_map/ppermute | solution.py:33
  207.2 19.2 %collective-permute-start.46 = (bf16[512,512]{1,0:T(8,128)(2,1)}, bf16[512,512]{1,0:T(8,128)(2,1)}, u32[]{:S(2)}, u32[]{:S(2)}) collective-permute-start(bf16[512,512]{1,0:T(8,128)(2,1)} %collective-permute-done.28.refs_4_.refs_10_), channel_id=1, source_target_pairs={{0,1},{1,2},{2,3},{3,0},{4,5},{5,6},{6,7},{7,4},{8,9},{9,10},{10,1... | collective-permute-start | bytes 1572872 | tf_op jit(solution)/shard_map/ppermute | solution.py:28
  221.3 14.7 %collective-permute-start.50 = (bf16[512,512]{1,0:T(8,128)(2,1)}, bf16[512,512]{1,0:T(8,128)(2,1)}, u32[]{:S(2)}, u32[]{:S(2)}) collective-permute-start(bf16[512,512]{1,0:T(8,128)(2,1)} %collective-permute-done.31.refs_5_.refs_12_), channel_id=1, source_target_pairs={{0,8},{4,12},{8,0},{12,4},{1,9},{5,13},{9,1},{13,5},{2,10},{6,14},... | collective-permute-start | bytes 1572872 | tf_op jit(solution)/shard_map/ppermute | solution.py:33
  222.3 15.2 %collective-permute-start.49 = (bf16[512,512]{1,0:T(8,128)(2,1)}, bf16[512,512]{1,0:T(8,128)(2,1)S(1)}, u32[]{:S(2)}, u32[]{:S(2)}) collective-permute-start(bf16[512,512]{1,0:T(8,128)(2,1)} %collective-permute-done.31.refs_5_.refs_12_), channel_id=1, source_target_pairs={{0,1},{1,2},{2,3},{3,0},{4,5},{5,6},{6,7},{7,4},{8,9},{9,10},{10,1... | collective-permute-start | bytes 1572872 | tf_op jit(solution)/shard_map/ppermute | solution.py:28
  228.4 18.8 %collective-permute-start.56 = (bf16[512,512]{1,0:T(8,128)(2,1)}, bf16[512,512]{1,0:T(8,128)(2,1)}, u32[]{:S(2)}, u32[]{:S(2)}) collective-permute-start(bf16[512,512]{1,0:T(8,128)(2,1)} %collective-permute-done.34.refs_0_.refs_3_), channel_id=1, source_target_pairs={{0,8},{4,12},{8,0},{12,4},{1,9},{5,13},{9,1},{13,5},{2,10},{6,14},... | collective-permute-start | bytes 1572872 | tf_op jit(solution)/shard_map/ppermute | solution.py:33
  229.4 19.5 %collective-permute-start.55 = (bf16[512,512]{1,0:T(8,128)(2,1)}, bf16[512,512]{1,0:T(8,128)(2,1)}, u32[]{:S(2)}, u32[]{:S(2)}) collective-permute-start(bf16[512,512]{1,0:T(8,128)(2,1)} %collective-permute-done.48.refs_6_), channel_id=1, source_target_pairs={{0,1},{1,2},{2,3},{3,0},{4,5},{5,6},{6,7},{7,4},{8,9},{9,10},{10,1... | collective-permute-start | bytes 1572872 | tf_op jit(solution)/shard_map/ppermute | solution.py:28
  243.8 20.7 %collective-permute-start.61 = (bf16[512,512]{1,0:T(8,128)(2,1)}, bf16[512,512]{1,0:T(8,128)(2,1)}, u32[]{:S(2)}, u32[]{:S(2)}) collective-permute-start(bf16[512,512]{1,0:T(8,128)(2,1)} %collective-permute-done.37.refs_1_.refs_5_), channel_id=1, source_target_pairs={{0,8},{4,12},{8,0},{12,4},{1,9},{5,13},{9,1},{13,5},{2,10},{6,14},... | collective-permute-start | bytes 1572872 | tf_op jit(solution)/shard_map/ppermute | solution.py:33
  244.4 20.2 %collective-permute-start.62 = (bf16[512,512]{1,0:T(8,128)(2,1)}, bf16[512,512]{1,0:T(8,128)(2,1)}, u32[]{:S(2)}, u32[]{:S(2)}) collective-permute-start(bf16[512,512]{1,0:T(8,128)(2,1)} %collective-permute-done.51.refs_6_), channel_id=1, source_target_pairs={{0,1},{1,2},{2,3},{3,0},{4,5},{5,6},{6,7},{7,4},{8,9},{9,10},{10,1... | collective-permute-start | bytes 1572872 | tf_op jit(solution)/shard_map/ppermute | solution.py:28
  248.9 26.5 %collective-permute-start.57 = (bf16[512,512]{1,0:T(8,128)(2,1)}, bf16[512,512]{1,0:T(8,128)(2,1)}, u32[]{:S(2)}, u32[]{:S(2)}) collective-permute-start(bf16[512,512]{1,0:T(8,128)(2,1)} %collective-permute-done.40.refs_2_.refs_7_), channel_id=1, source_target_pairs={{0,8},{4,12},{8,0},{12,4},{1,9},{5,13},{9,1},{13,5},{2,10},{6,14},... | collective-permute-start | bytes 1572872 | tf_op jit(solution)/shard_map/ppermute | solution.py:33
  249.6 25.8 %collective-permute-start.58 = (bf16[512,512]{1,0:T(8,128)(2,1)}, bf16[512,512]{1,0:T(8,128)(2,1)}, u32[]{:S(2)}, u32[]{:S(2)}) collective-permute-start(bf16[512,512]{1,0:T(8,128)(2,1)} %collective-permute-done.50.refs_6_), channel_id=1, source_target_pairs={{0,1},{1,2},{2,3},{3,0},{4,5},{5,6},{6,7},{7,4},{8,9},{9,10},{10,1... | collective-permute-start | bytes 1572872 | tf_op jit(solution)/shard_map/ppermute | solution.py:28
  252.3 12.3 %collective-permute-start.60 = (bf16[512,1024]{1,0:T(8,128)(2,1)}, bf16[512,1024]{1,0:T(8,128)(2,1)}, u32[]{:S(2)}, u32[]{:S(2)}) collective-permute-start(bf16[512,1024]{1,0:T(8,128)(2,1)} %maximum_select_fusion), channel_id=1, source_target_pairs={{0,4},{4,0},{8,12},{12,8},{1,5},{5,1},{9,13},{13,9},{2,6},{6,2},{1... | collective-permute-start | bytes 3145736 | tf_op jit(solution)/shard_map/ppermute | solution.py:33
  (35 other events, 283.0 us)
